TPU v7x, 256 devices: a whole 4x4x8 slice. The times are simulated.
256 devices in a mesh: texel: 16 (over x, y), light: 4 (over z_hi), view: 4 (over z_lo, core).
Axes of the slice: x: 4, y: 4, z: 8 (z_hi: 4, z_lo: 2; z = z_hi * 2 + z_lo), core: 2. Of those that a mesh axis runs over, the one named last changes fastest.
Arguments:
- slab: bfloat16 [80, 80, 16384], P('light', 'view', 'texel'), may hold values from -6 to 6
- basis: bfloat16 [80, 48], P('view'), may hold values from -0.625 to 0.625
Outputs:
- view_gram: float32 [80, 80], P('view')
- core: bfloat16 [48, 80, 16384], P('view', 'light', 'texel')
- light_gram: float32 [80, 80], P('light')
All inputs are finite; a program needn't handle non-finite values.
Results may differ from a plain program's by a relative error of at most 0.001.
Values may be sent and summed in bfloat16 or wider, within the bound.
A program may use at most 64 MiB of HBM per device.

v0:
```python
import jax
import jax.numpy as jnp
from jax import lax
from jax.sharding import PartitionSpec as P


def row_total(partial_value):
    return lax.psum(partial_value, ("texel", "light"))


def body(slab, basis):
    lights_dev, views_dev, columns_dev = slab.shape
    ranks = basis.shape[1]
    light_count = lights_dev * lax.axis_size("light")
    columns_all = columns_dev * lax.axis_size("texel")
    view_scale = 1.0 / (light_count * columns_all)
    block = jnp.einsum(
        "lvc,lwc->vw",
        slab,
        lax.all_gather(slab, "view", axis=1, tiled=True),
        preferred_element_type=jnp.float32,
    )
    partial_value = block
    view_gram = row_total(partial_value * view_scale)
    core_sum = lax.psum_scatter(
        jnp.einsum("vr,lvc->rlc", basis, slab, preferred_element_type=jnp.float32),
        "view",
        scatter_dimension=0,
        tiled=True,
    )
    core = core_sum.astype(jnp.bfloat16)
    light_scale = 1.0 / (ranks * columns_all)
    block = jnp.einsum(
        "rlc,rmc->lm",
        core,
        lax.all_gather(core, "light", axis=1, tiled=True),
        preferred_element_type=jnp.float32,
    )
    light_gram = lax.psum(block * light_scale, ("texel", "view"))
    return (view_gram, core, light_gram)


def solution(mesh):
    return jax.shard_map(
        body,
        mesh=mesh,
        in_specs=(P("light", "view", "texel"), P("view", None)),
        out_specs=(P("view", None), P("view", "light", "texel"), P("light", None)),
        check_vma=False,
    )
```

profile of v0, /device:TPU:1, one launch (start us, length us, event | category | flops | bytes accessed | tf_op | source)
XLA Modules:
  0.0 784.8 jit_solution(6332174466375986742)
XLA Ops:
  7.2 0.0 copy-start
  7.2 0.0 reduce-scatter.2.cloned.1.call-start
  7.2 0.6 copy-done
  7.9 1.9 fusion.16
  9.8 4.4 copy.10
  14.2 0.0 copy-start.1
  14.2 0.0 reduce-scatter.2.cloned.1.call-update
  14.2 0.0 all-gather.3.cloned.1.call-start
  14.3 1.1 copy-done.1
  15.4 1.4 copy.8
  16.8 0.0 all-gather.3.cloned.1.call-update
  16.9 0.0 all-gather.5.cloned.1.call-start
  16.9 53.8 %reduce-scatter.2.cloned.1.call-done = f32[12,20,1024]{2,1,0:T(8,128)} async-done(((f32[48,20,1024]{2,1,0:T(8,128)}), f32[12,20,1024]{2,1,0:T(8,128)}) %reduce-scatter.2.cloned.1.call-update) | async-done | bytes 983056 | tf_op jit(solution)/shard_map/reduce_scatter | solution.py:25
  70.7 1.4 convert_element_type.3
  72.1 0.0 copy-start.2
  72.1 1.2 copy.11
  73.3 0.0 all-gather.5.cloned.1.call-update
  73.3 46.8 %all-gather.3.cloned.1.call-done = bf16[20,80,1024]{2,0,1:T(8,128)(2,1)} async-done(((bf16[20,20,1024]{2,0,1:T(8,128)(2,1)}), bf16[20,80,1024]{2,0,1:T(8,128)(2,1)}) %all-gather.3.cloned.1.call-update) | async-done | bytes 3276816 | tf_op jit(solution)/shard_map/all_gather | solution.py:20
  120.1 5.9 fusion.10
  126.0 326.3 %psum.14 = f32[20,80]{1,0:T(8,128)} all-reduce(f32[20,80]{1,0:T(8,128)S(1)} %fusion.10), channel_id=1, replica_groups=mesh['texel'=16,'light'=4,'view'=4] {'texel','light'}, use_global_device_ids=true, to_apply=%region_0.0 | all-reduce | flops 1600 | bytes 12800 | tf_op jit(solution)/shard_map/psum | solution.py:8
  452.3 0.0 all-gather.5.cloned.1.call-done
  452.3 4.0 fusion.13
  456.3 0.0 copy-done.2
  456.3 321.9 %psum.15 = f32[20,80]{1,0:T(8,128)} all-reduce(f32[20,80]{1,0:T(8,128)S(1)} %fusion.13), channel_id=1, replica_groups=mesh['texel'=16,'light'=4,'view'=4] {'texel','view'}, use_global_device_ids=true, to_apply=%region_2.0 | all-reduce | flops 1600 | bytes 12800 | tf_op jit(solution)/shard_map/psum | solution.py:39
Async XLA Ops:
  7.2 0.7 copy-start
  7.2 63.6 %reduce-scatter.2.cloned.1.call-start = ((), (), s32[]{:S(2)}) async-start(), calls=%async_computation.2 | async-start | bytes 5898240 | tf_op jit(solution)/shard_map/reduce_scatter | solution.py:25
  14.2 1.2 copy-start.1
  14.2 105.9 %all-gather.3.cloned.1.call-start = ((), (), s32[]{:S(2)}) async-start(), calls=%async_computation.1 | async-start | bytes 4915200 | tf_op jit(solution)/shard_map/all_gather | solution.py:20
  16.9 435.4 %all-gather.5.cloned.1.call-start = ((), (), s32[]{:S(2)}) async-start(), calls=%async_computation.3 | async-start | bytes 3276800 | tf_op jit(solution)/shard_map/all_gather | solution.py:36
  72.1 384.2 %copy-start.2 = (bf16[12,20,1024]{2,1,0:T(8,128)(2,1)}, bf16[12,20,1024]{2,1,0:T(8,128)(2,1)S(1)}, u32[]{:S(2)}) copy-start(bf16[12,20,1024]{2,1,0:T(8,128)(2,1)S(1)} %convert_element_type.3) | copy-start | bytes 1474564
Sparse Core Ops, SparseCore 0:
  14.3 56.3 reduce-scatter.1
  72.5 47.5 all-gather.2
  121.9 59.2 all-gather.4
where the time goes:
time: 788 us; the launch traced here: 785 us
  blocking collectives  648 us (82%)
  waiting for transfers between devices  101 us (13%)
  between operations  13.8 us (2%)
  matrix products  11.8 us (1%)
  local copies, waits for them, and re-layouts  8.85 us (1%)
    psum x1, blocking collectives, row_total(): return lax.psum(partial_value, ('texel', 'light'))  326 us
    psum x1, blocking collectives, body(): light_gram = lax.psum(block * light_scale, ('texel', 'view'))  322 us
    reduce_scatter x1, waiting for transfers between devices, body(): lax.psum_scatter(jnp.einsum('vr,lvc->rlc', basis, slab, preferred_element...  53.8 us
    all_gather x1, waiting for transfers between devices, body(): lax.all_gather(slab, 'view', axis=1, tiled=True)  46.8 us
  transfers between devices with their start and end apart: 3, of which 2 were waited for; matrix products, arithmetic and copies ran while one was open for 1% of the time, Pallas kernels for 0%

commit v1 on v0

v1 whole, which is shorter than its diff:
```python
import functools

import jax
import jax.numpy as jnp
import numpy as np
from jax import lax
from jax.experimental import pallas as pl
from jax.experimental.pallas import tpu as pltpu
from jax.sharding import PartitionSpec as P

MESH = pl.DeviceIdType.MESH
BF = jnp.bfloat16
F32 = jnp.float32
LB = 20
VB = 20
NV = 4
NL = 4
RB = 12
CB = 256
ROWS = LB * VB
PIECE = RB * LB
GROUP = 80
PAGES = NL * NV


def constants():
    expand = np.zeros((NV * 32, NV * ROWS), np.float32)
    for s in range(NV):
        for l in range(LB):
            for v in range(VB):
                expand[s * 32 + v, s * ROWS + l * VB + v] = 1
    spread = np.zeros((NV * PIECE, 128), np.float32)
    for r in range(NV * RB):
        spread[r * LB : (r + 1) * LB, r] = 1
    rows = np.arange(GROUP)[:, None] % LB
    columns = (np.arange(NV * ROWS)[None, :] // VB) % LB
    mask = (rows == columns).astype(np.float32)
    index = np.arange(4 * GROUP)
    repeat = (index // 20) % 4
    keep = (repeat[:, None] == repeat[None, :]).astype(np.float32)
    item = (index // GROUP) * 20 + index % 20
    pick = np.zeros((2, 8 * PAGES, 4 * GROUP), np.float32)
    for p in range(PAGES):
        for q in range(5):
            pick[0, 8 * p + q] = item == 5 * (NL * (p % NV) + p // NV) + q
            pick[1, 8 * p + q] = item == 5 * p + q
    gather = (item[:, None] == np.arange(128)[None, :]).astype(np.float32)
    return expand, spread, mask, keep, pick, gather


def odd_share(k, t):
    return lax.rem(lax.div(k + 1 - t, 2), 2)


def share_of(k, j):
    e, t = lax.div(j, 2), lax.rem(j, 2)
    return 2 * t + lax.rem(odd_share(k, t) + 1 - e, 2)


def member_for(k, b):
    t, u = lax.div(b, 2), lax.rem(b, 2)
    return 2 * lax.rem(odd_share(k, t) + 1 + u, 2) + t


def center_of(b, n):
    t, u = lax.div(b, 2), lax.rem(b, 2)
    z = lax.rem(1 + 4 * u + 2 * t + lax.div(n, 2), 8)
    return lax.div(z, 2), 2 * lax.rem(z, 2) + lax.rem(n, 2)


def split_dot(a, b):
    def parts(x):
        hi = x.astype(BF)
        rest = x - hi.astype(F32)
        mid = rest.astype(BF)
        return hi, mid, (rest - mid.astype(F32)).astype(BF)

    if a.dtype == BF:
        return sum(jnp.dot(a, p, preferred_element_type=F32) for p in parts(b))
    return sum(jnp.dot(p, b, preferred_element_type=F32) for p in parts(a))


def kernel(
    view_scale, light_scale,
    slab_ref, basis_ref, expand_ref, spread_ref, mask_ref, keep_ref, pick_ref, gather_ref,
    view_ref, core_ref, light_ref,
    dense, share, own_basis, all_basis, weights, pieces, core_land, light_land,
    pages, pages_land, part, part_land, last, last_view, last_light,
    basis_send, basis_recv, slab_send, slab_recv, core_send, core_recv,
    light_send, light_recv, z_send, z_recv, t_send, t_recv, v_send, v_recv, l_send, l_recv,
):
    texels = lax.axis_size("texel")
    tex, i, j = lax.axis_index("texel"), lax.axis_index("light"), lax.axis_index("view")
    me = i * NV + j
    mine = share_of(i, j)

    barrier = pltpu.get_barrier_semaphore()

    def greet_z(o, c):
        other = lax.rem(me + o, PAGES)
        pl.semaphore_signal(
            barrier, inc=1, device_id=(tex, lax.div(other, NV), lax.rem(other, NV)), device_id_type=MESH
        )
        return c

    def greet_t(o, c):
        pl.semaphore_signal(barrier, inc=1, device_id=(lax.rem(tex + o, texels), i, j), device_id_type=MESH)
        return c

    lax.fori_loop(1, PAGES, greet_z, 0)
    lax.fori_loop(1, texels, greet_t, 0)

    own_basis[...] = jnp.zeros_like(own_basis)
    own_basis[0:VB, 0 : NV * RB] = basis_ref[...]
    for l in range(LB):
        dense[l * VB : (l + 1) * VB, :] = slab_ref[l]

    pl.semaphore_wait(barrier, PAGES - 1 + texels - 1)

    def remote(src, dst, send, recv, device):
        return pltpu.make_async_remote_copy(
            src_ref=src, dst_ref=dst, send_sem=send, recv_sem=recv, device_id=device, device_id_type=MESH
        )

    sends = []
    for o in (2, 3, 1):
        other = lax.rem(j + o, NV)
        sends.append(remote(own_basis, all_basis.at[j], basis_send.at[o], basis_recv.at[j], (tex, i, other)))
        sends[-1].start()
    for o in (2, 3, 1):
        other = lax.rem(j + o, NV)
        columns = pl.ds(pl.multiple_of(share_of(i, other) * CB, CB), CB)
        sends.append(
            remote(
                dense.at[:, columns], share.at[pl.ds(pl.multiple_of(j * ROWS, 16), ROWS), :],
                slab_send.at[o], slab_recv.at[j], (tex, i, other),
            )
        )
        sends[-1].start()
    columns = pl.ds(pl.multiple_of(mine * CB, CB), CB)
    local = pltpu.make_async_copy(
        dense.at[:, columns], share.at[pl.ds(pl.multiple_of(j * ROWS, 16), ROWS), :], slab_recv.at[j]
    )
    local.start()
    all_basis[j] = own_basis[...]
    for o in (1, 2, 3):
        other = lax.rem(j + o, NV)
        remote(
            own_basis, all_basis.at[other], basis_send.at[o], basis_recv.at[other], (tex, i, other)
        ).wait_recv()

    stacked = all_basis[...].reshape(NV * 32, 128)
    table = lax.dot_general(
        stacked, expand_ref[...], (((0,), (0,)), ((), ())), preferred_element_type=F32
    ).astype(BF)

    def weight_rows(g, c):
        at = pl.ds(pl.multiple_of(g * GROUP, 16), GROUP)
        full = jnp.dot(spread_ref[at, :], table, preferred_element_type=F32)
        weights[at, :] = full.astype(BF) * mask_ref[...]
        return c

    lax.fori_loop(0, NV * PIECE // GROUP, weight_rows, 0)

    local.wait()
    for o in (1, 2, 3):
        other = lax.rem(j + o, NV)
        at = pl.ds(pl.multiple_of(other * ROWS, 16), ROWS)
        remote(
            dense.at[:, columns], share.at[at, :], slab_send.at[o], slab_recv.at[other], (tex, i, other)
        ).wait_recv()

    for o in (2, 3, 1, 0):
        p = lax.rem(j + o, NV)
        at = pl.ds(pl.multiple_of(p * PIECE, 16), PIECE)
        pieces[at, :] = jnp.dot(weights[at, :], share[...], preferred_element_type=F32).astype(BF)
        ci, cj = center_of(mine, p)
        here = jnp.logical_and(ci == i, cj == j)

        @pl.when(here)
        def _():
            pltpu.make_async_copy(pieces.at[at, :], light_land.at[i], light_recv.at[i]).start()

        @pl.when(jnp.logical_not(here))
        def _():
            remote(pieces.at[at, :], light_land.at[i], light_send.at[o], light_recv.at[i], (tex, ci, cj)).start()

        if o:
            copy = remote(
                pieces.at[at, :], core_land.at[:, columns], core_send.at[o], core_recv.at[j], (tex, i, p)
            )
            sends.append(copy)
        else:
            copy = pltpu.make_async_copy(pieces.at[at, :], core_land.at[:, columns], core_recv.at[j])
        copy.start()

    def gram(blocks, which):
        total = None
        for block in blocks:
            term = lax.dot_general(block, block, (((1,), (1,)), ((), ())), preferred_element_type=F32)
            total = term if total is None else total + term
        rows = split_dot(pick_ref[which], total * keep_ref[...])
        return split_dot(rows, gather_ref[...])

    view_part = gram(
        (jnp.concatenate([share[s * ROWS + g * GROUP : s * ROWS + (g + 1) * GROUP, :] for s in range(NV)], axis=0)
        for g in range(ROWS // GROUP)), 0
    )
    pages[:, 0:8, :] = view_part.reshape(PAGES, 8, 128)

    for k in range(NL):
        pltpu.make_async_copy(pieces.at[pl.ds(0, PIECE), :], light_land.at[k], light_recv.at[k]).wait()
    light_part = gram(
        (jnp.concatenate([light_land[k, g * GROUP : (g + 1) * GROUP, :] for k in range(NL)], axis=0)
        for g in range(PIECE // GROUP)), 1
    )
    pages[:, 8:16, :] = light_part.reshape(PAGES, 8, 128)

    def z_copy(o, slot):
        other = lax.rem(me + o, PAGES)
        return remote(
            pages.at[other], pages_land.at[slot(other)], z_send.at[o], z_recv.at[slot(other)],
            (tex, lax.div(other, NV), lax.rem(other, NV)),
        )

    def z_start(o, c):
        z_copy(o, lambda other: me).start()
        return c

    def z_wait(o, c):
        z_copy(o, lambda other: other).wait_recv()
        return c

    lax.fori_loop(1, PAGES, z_start, 0)
    pages_land[me] = pages[me]
    lax.fori_loop(1, PAGES, z_wait, 0)
    part[...] = jnp.sum(pages_land[...], axis=0)

    def t_copy(o, slot):
        other = lax.rem(tex + o, texels)
        return remote(part, part_land.at[slot(other)], t_send.at[o], t_recv.at[slot(other)], (other, i, j))

    def t_start(o, c):
        t_copy(o, lambda other: tex).start()
        return c

    def t_wait(o, c):
        t_copy(o, lambda other: other).wait_recv()
        return c

    lax.fori_loop(1, texels, t_start, 0)
    part_land[tex] = part[...]
    lax.fori_loop(1, texels, t_wait, 0)
    last[...] = jnp.sum(part_land[...], axis=0)

    def v_copy(o, slot):
        other = lax.rem(i + o, NL)
        return remote(last.at[0:8], last_view.at[slot(other)], v_send.at[o], v_recv.at[slot(other)], (tex, other, j))

    def l_copy(o, slot):
        other = lax.rem(j + o, NV)
        return remote(
            last.at[8:16], last_light.at[slot(other)], l_send.at[o], l_recv.at[slot(other)], (tex, i, other)
        )

    for o in (1, 2, 3):
        v_copy(o, lambda other: i).start()
        l_copy(o, lambda other: j).start()
    last_view[i] = last[0:8]
    last_light[j] = last[8:16]

    pltpu.make_async_copy(pieces.at[pl.ds(0, PIECE), :], core_land.at[:, columns], core_recv.at[j]).wait()
    for o in (1, 2, 3):
        other = lax.rem(j + o, NV)
        theirs = pl.ds(pl.multiple_of(share_of(i, other) * CB, CB), CB)
        remote(
            pieces.at[pl.ds(0, PIECE), :], core_land.at[:, theirs], core_send.at[o], core_recv.at[other],
            (tex, i, other),
        ).wait_recv()
    core_ref[...] = core_land[...]

    for o in (1, 2, 3):
        v_copy(o, lambda other: other).wait_recv()
        l_copy(o, lambda other: other).wait_recv()
    for q in range(4):
        view_ref[5 * q : 5 * q + 5, :] = last_view[q, 0:5, 0:80] * view_scale
        light_ref[5 * q : 5 * q + 5, :] = last_light[q, 0:5, 0:80] * light_scale

    for copy in sends:
        copy.wait_send()
    for o in range(NV):
        p = lax.rem(j + o, NV)
        ci, cj = center_of(mine, p)
        at = pl.ds(pl.multiple_of(p * PIECE, 16), PIECE)

        @pl.when(jnp.logical_not(jnp.logical_and(ci == i, cj == j)))
        def _():
            remote(
                pieces.at[at, :], light_land.at[i], light_send.at[o], light_recv.at[i], (tex, ci, cj)
            ).wait_send()

    def send_waits(o, c):
        z_copy(o, lambda other: me).wait_send()
        t_copy(o, lambda other: tex).wait_send()
        return c

    lax.fori_loop(1, PAGES, send_waits, 0)
    for o in (1, 2, 3):
        v_copy(o, lambda other: i).wait_send()
        l_copy(o, lambda other: j).wait_send()


def body(slab, basis):
    texels = lax.axis_size("texel")
    columns_all = slab.shape[2] * texels
    view_scale = 1.0 / (LB * NL * columns_all)
    light_scale = 1.0 / (RB * NV * columns_all)
    tables = constants()
    tables = [jnp.asarray(x, F32 if n == 3 else BF) for n, x in enumerate(tables)]
    vmem = pl.BlockSpec(memory_space=pltpu.VMEM)
    dma = pltpu.SemaphoreType.DMA
    view_gram, core, light_gram = pl.pallas_call(
        functools.partial(kernel, view_scale, light_scale),
        out_shape=(
            jax.ShapeDtypeStruct((VB, 80), F32),
            jax.ShapeDtypeStruct((PIECE, 4 * CB), BF),
            jax.ShapeDtypeStruct((LB, 80), F32),
        ),
        in_specs=[vmem] * 8,
        out_specs=(vmem,) * 3,
        scratch_shapes=[
            pltpu.VMEM((ROWS, 4 * CB), BF),
            pltpu.VMEM((NV * ROWS, CB), BF),
            pltpu.VMEM((32, 128), BF),
            pltpu.VMEM((NV, 32, 128), BF),
            pltpu.VMEM((NV * PIECE, NV * ROWS), BF),
            pltpu.VMEM((NV * PIECE, CB), BF),
            pltpu.VMEM((PIECE, 4 * CB), BF),
            pltpu.VMEM((NL, PIECE, CB), BF),
            pltpu.VMEM((PAGES, 16, 128), F32),
            pltpu.VMEM((PAGES, 16, 128), F32),
            pltpu.VMEM((16, 128), F32),
            pltpu.VMEM((texels, 16, 128), F32),
            pltpu.VMEM((16, 128), F32),
            pltpu.VMEM((NL, 8, 128), F32),
            pltpu.VMEM((NV, 8, 128), F32),
            dma((NV,)), dma((NV,)), dma((NV,)), dma((NV,)), dma((NV,)), dma((NV,)),
            dma((NV,)), dma((NL,)), dma((PAGES,)), dma((PAGES,)), dma((texels,)), dma((texels,)),
            dma((NL,)), dma((NL,)), dma((NV,)), dma((NV,)),
        ],
        compiler_params=pltpu.CompilerParams(
            collective_id=0, has_side_effects=True, vmem_limit_bytes=48 * 1024 * 1024
        ),
    )(slab, basis, *tables)
    return view_gram, core.reshape(RB, LB, 4 * CB), light_gram


def solution(mesh):
    return jax.shard_map(
        body,
        mesh=mesh,
        in_specs=(P("light", "view", "texel"), P("view", None)),
        out_specs=(P("view", None), P("view", "light", "texel"), P("light", None)),
        check_vma=False,
    )
```

time: 788 us -> 62.5 us (0.08)
  blocking collectives: 648 us -> 0 us
  waiting for transfers between devices: 101 us -> 0 us
  Pallas kernels: 0 us -> 51.7 us
  between operations: 13.8 us -> 0.65 us
  matrix products: 11.8 us -> 0 us
    psum x2 -> x0, blocking collectives: 648 us -> none  [the longest x1 326 us: row_total(): return lax.psum(partial_value, ('texel', 'light'))]
    reduce_scatter x1 -> x0, waiting for transfers between devices: 53.8 us -> none  [body(): lax.psum_scatter(jnp.einsum('vr,lvc->rlc', basis, slab, preferred_element...]
    pallas_call x0 -> x1, Pallas kernels: none -> 51.7 us  [body(): pl.pallas_call(functools.partial(kernel, view_scale, light_scale), out_sh...]
    all_gather x2 -> x0, waiting for transfers between devices: 46.8 us -> none  [the longest x1 46.8 us: body(): lax.all_gather(slab, 'view', axis=1, tiled=True)]
    dot_general x3 -> x0, matrix products: 11.8 us -> none  [the longest x1 5.85 us: body(): jnp.einsum('lvc,lwc->vw', slab, lax.all_gather(slab, 'view', axis=1, tile...]
  transfers between devices with their start and end apart: 3 -> 0, of which waited for: 2 -> 0; matrix products, arithmetic and copies ran while one was open for 1% -> 0% of each run, Pallas kernels for 0% -> 0%
where the time goes in v1:
time: 62.5 us; the launch traced here: 62.1 us
  Pallas kernels  51.7 us (83%)
  local copies, waits for them, and re-layouts  9.74 us (16%)
  between operations  0.65 us (1%)
    pallas_call x1, Pallas kernels, body(): pl.pallas_call(functools.partial(kernel, view_scale, light_scale), out_sh...  51.7 us
    unnamed x18, local copies, waits for them, and re-layouts  8.83 us

profile of v1, /device:TPU:1, one launch (start us, length us, event | category | flops | bytes accessed | tf_op | source)
XLA Modules:
  0.0 62.1 jit_solution(1229702987617753555)
XLA Ops:
  0.6 0.0 copy-start
  0.6 1.2 %copy-done = bf16[20,20,1024]{2,1,0:T(8,128)(2,1)S(1)} copy-done((bf16[20,20,1024]{2,1,0:T(8,128)(2,1)S(1)}, bf16[20,20,1024]{2,1,0:T(8,128)(2,1)}, u32[]{:S(2)}) %copy-start) | copy-done | bytes 819224
  1.8 0.0 copy-start.1
  1.8 1.0 %copy-done.1 = f32[320,320]{1,0:T(8,128)S(1)} copy-done((f32[320,320]{1,0:T(8,128)S(1)}, f32[320,320]{1,0:T(8,128)}, u32[]{:S(2)}) %copy-start.1) | copy-done | bytes 409624
  2.9 0.0 copy-start.2
  2.9 1.0 %copy-done.2 = bf16[128,1600]{1,0:T(8,128)(2,1)S(1)} copy-done((bf16[128,1600]{1,0:T(8,128)(2,1)S(1)}, bf16[128,1600]{1,0:T(8,128)(2,1)}, u32[]{:S(2)}) %copy-start.2) | copy-done | bytes 409624
  3.9 0.0 copy-start.3
  3.9 0.9 %copy-done.3 = bf16[80,1600]{1,0:T(8,128)(2,1)S(1)} copy-done((bf16[80,1600]{1,0:T(8,128)(2,1)S(1)}, bf16[80,1600]{1,0:T(8,128)(2,1)}, u32[]{:S(2)}) %copy-start.3) | copy-done | bytes 256024
  4.8 0.0 copy-start.4
  4.8 0.9 %copy-done.4 = bf16[960,128]{1,0:T(8,128)(2,1)S(1)} copy-done((bf16[960,128]{1,0:T(8,128)(2,1)S(1)}, bf16[960,128]{1,0:T(8,128)(2,1)}, u32[]{:S(2)}) %copy-start.4) | copy-done | bytes 245784
  5.8 0.0 copy-start.5
  5.8 0.9 %copy-done.5 = bf16[2,128,320]{2,1,0:T(8,128)(2,1)S(1)} copy-done((bf16[2,128,320]{2,1,0:T(8,128)(2,1)S(1)}, bf16[2,128,320]{2,1,0:T(8,128)(2,1)}, u32[]{:S(2)}) %copy-start.5) | copy-done | bytes 163864
  6.7 0.0 copy-start.6
  6.7 0.9 %copy-done.6 = bf16[320,128]{1,0:T(8,128)(2,1)S(1)} copy-done((bf16[320,128]{1,0:T(8,128)(2,1)S(1)}, bf16[320,128]{1,0:T(8,128)(2,1)}, u32[]{:S(2)}) %copy-start.6) | copy-done | bytes 81944
  7.6 0.0 copy-start.7
  7.6 0.7 %copy-done.7 = bf16[20,48]{1,0:T(8,128)(2,1)S(1)} copy-done((bf16[20,48]{1,0:T(8,128)(2,1)S(1)}, bf16[20,48]{1,0:T(8,128)(2,1)}, u32[]{:S(2)}) %copy-start.7) | copy-done | bytes 1944
  8.3 51.7 %shard_map.103 = (f32[20,80]{1,0:T(8,128)S(1)}, bf16[240,1024]{1,0:T(8,128)(2,1)S(1)}, f32[20,80]{1,0:T(8,128)S(1)}) custom-call(bf16[20,20,1024]{2,1,0:T(8,128)(2,1)S(1)} %copy-done, bf16[20,48]{1,0:T(8,128)(2,1)S(1)} %copy-done.7, bf16[128,1600]{1,0:T(8,128)(2,1)S(1)} %copy-done.2, bf16[960,128]{1,0:T(8,128)(2,1)S(1)} %copy-done.4, ...), custom_call_target="tpu_custom_call" | custom-call | tf_op jit(solution)/shard_map/pallas_call | solution.py:322
  60.0 0.9 %reshape.9 = bf16[12,20,1024]{2,1,0:T(8,128)(2,1)} reshape(bf16[240,1024]{1,0:T(8,128)(2,1)S(1)} %get-tuple-element.7) | data formatting | bytes 983040 | tf_op jit(solution)/shard_map/reshape | solution.py:355
  60.9 0.6 copy.13
  61.5 0.6 copy.14
Async XLA Ops:
  0.6 1.2 %copy-start = (bf16[20,20,1024]{2,1,0:T(8,128)(2,1)S(1)}, bf16[20,20,1024]{2,1,0:T(8,128)(2,1)}, u32[]{:S(2)}) copy-start(bf16[20,20,1024]{2,1,0:T(8,128)(2,1)} %slab_ref.1) | copy-start | bytes 2457604
  1.8 1.0 %copy-start.1 = (f32[320,320]{1,0:T(8,128)S(1)}, f32[320,320]{1,0:T(8,128)}, u32[]{:S(2)}) copy-start(f32[320,320]{1,0:T(8,128)} %constant.15.clone.keep_ref) | copy-start | bytes 1228804
  2.9 1.0 %copy-start.2 = (bf16[128,1600]{1,0:T(8,128)(2,1)S(1)}, bf16[128,1600]{1,0:T(8,128)(2,1)}, u32[]{:S(2)}) copy-start(bf16[128,1600]{1,0:T(8,128)(2,1)} %constant.12.clone.expand_ref) | copy-start | bytes 1228804
  3.9 1.0 %copy-start.3 = (bf16[80,1600]{1,0:T(8,128)(2,1)S(1)}, bf16[80,1600]{1,0:T(8,128)(2,1)}, u32[]{:S(2)}) copy-start(bf16[80,1600]{1,0:T(8,128)(2,1)} %constant.14.clone.mask_ref) | copy-start | bytes 768004
  4.8 0.9 %copy-start.4 = (bf16[960,128]{1,0:T(8,128)(2,1)S(1)}, bf16[960,128]{1,0:T(8,128)(2,1)}, u32[]{:S(2)}) copy-start(bf16[960,128]{1,0:T(8,128)(2,1)} %constant.13.clone.spread_ref) | copy-start | bytes 737284
  5.8 0.9 %copy-start.5 = (bf16[2,128,320]{2,1,0:T(8,128)(2,1)S(1)}, bf16[2,128,320]{2,1,0:T(8,128)(2,1)}, u32[]{:S(2)}) copy-start(bf16[2,128,320]{2,1,0:T(8,128)(2,1)} %constant.16.clone.pick_ref) | copy-start | bytes 491524
  6.7 0.9 %copy-start.6 = (bf16[320,128]{1,0:T(8,128)(2,1)S(1)}, bf16[320,128]{1,0:T(8,128)(2,1)}, u32[]{:S(2)}) copy-start(bf16[320,128]{1,0:T(8,128)(2,1)} %constant.17.clone.gather_ref) | copy-start | bytes 245764
  7.6 0.7 %copy-start.7 = (bf16[20,48]{1,0:T(8,128)(2,1)S(1)}, bf16[20,48]{1,0:T(8,128)(2,1)}, u32[]{:S(2)}) copy-start(bf16[20,48]{1,0:T(8,128)(2,1)} %basis_ref.1) | copy-start | bytes 5764

commit v2 on v0

v2 whole, which is shorter than its diff:
```python
import functools

import jax
import jax.numpy as jnp
from jax import lax
from jax.experimental import pallas as pl
from jax.experimental.pallas import tpu as pltpu
from jax.sharding import PartitionSpec as P

MESH = pl.DeviceIdType.MESH
BF = jnp.bfloat16
F32 = jnp.float32
LB = 20
VB = 20
NV = 4
NL = 4
RB = 12
CB = 256
HB = CB // 2
ROWS = LB * VB
PIECE = RB * LB
GROUP = 80
PAGES = NL * NV


def cells(shape):
    return lax.broadcasted_iota(jnp.int32, shape, 0), lax.broadcasted_iota(jnp.int32, shape, 1)


def div20(x):
    return (x * 3277) >> 16


def ones_where(condition, dtype=BF):
    return jnp.where(condition, 1.0, 0.0).astype(dtype)


def expand_table():
    row, col = cells((NV * 32, NV * ROWS))
    line = div20(col)
    return ones_where(row == 32 * div20(line) + col - VB * line)


def light_mask():
    row, col = cells((GROUP, NV * ROWS))
    line = div20(col)
    return ones_where(row - LB * div20(row) == line - LB * div20(line))


def spread_rows(g):
    row, col = cells((GROUP, 128))
    return ones_where(div20(row) + 4 * g == col)


def item(x):
    line = div20(x)
    return 20 * (line >> 2) + x - 20 * line


def keep_table():
    row, col = cells((4 * GROUP, 4 * GROUP))
    return (div20(row) & 3) == (div20(col) & 3)


def pick_table(turned):
    row, col = cells((8 * PAGES, 4 * GROUP))
    p, q = row >> 3, row & 7
    if turned:
        p = NL * (p & 3) + (p >> 2)
    return ones_where((q < 5) & (5 * p + q == item(col)))


def gather_table():
    row, col = cells((4 * GROUP, 128))
    return ones_where(item(row) == col)


def odd_share(k, t):
    return lax.rem(lax.div(k + 1 - t, 2), 2)


def share_of(k, j):
    e, t = lax.div(j, 2), lax.rem(j, 2)
    return 2 * t + lax.rem(odd_share(k, t) + 1 - e, 2)


def member_for(k, b):
    t, u = lax.div(b, 2), lax.rem(b, 2)
    return 2 * lax.rem(odd_share(k, t) + 1 + u, 2) + t


def center_of(b, n):
    t, u = lax.div(b, 2), lax.rem(b, 2)
    z = lax.rem(1 + 4 * u + 2 * t + lax.div(n, 2), 8)
    return lax.div(z, 2), 2 * lax.rem(z, 2) + lax.rem(n, 2)


def split_dot(a, b):
    def parts(x):
        hi = x.astype(BF)
        rest = x - hi.astype(F32)
        mid = rest.astype(BF)
        return hi, mid, (rest - mid.astype(F32)).astype(BF)

    if a.dtype == BF:
        return sum(jnp.dot(a, p, preferred_element_type=F32) for p in parts(b))
    return sum(jnp.dot(p, b, preferred_element_type=F32) for p in parts(a))


def remote(src, dst, send, recv, device):
    return pltpu.make_async_remote_copy(
        src_ref=src, dst_ref=dst, send_sem=send, recv_sem=recv, device_id=device, device_id_type=MESH
    )


def kernel(
    view_scale, light_scale,
    slab_hbm, basis_hbm,
    view_ref, core_ref, light_ref,
    slab_ref, basis_ref, mask_ref, dense, share, own_basis, all_basis, weights, pieces, core_land, light_land,
    pages, z_land, part, t_land, whole, last_land,
    load, basis_send, basis_recv, slab_send, slab_recv, core_send, core_recv,
    light_send, light_recv, z_send, z_recv, t_send, t_recv, last_send, last_recv,
):
    texels = lax.axis_size("texel")
    tex, i, j = lax.axis_index("texel"), lax.axis_index("light"), lax.axis_index("view")
    me = i * NV + j
    mine = share_of(i, j)

    load_slab = pltpu.make_async_copy(slab_hbm, slab_ref, load.at[0])
    load_basis = pltpu.make_async_copy(basis_hbm, basis_ref, load.at[1])
    load_slab.start()
    load_basis.start()
    barrier = pltpu.get_barrier_semaphore()

    def greet_z(o, c):
        other = lax.rem(me + o, PAGES)
        pl.semaphore_signal(
            barrier, inc=1, device_id=(tex, lax.div(other, NV), lax.rem(other, NV)), device_id_type=MESH
        )
        return c

    def greet_t(o, c):
        pl.semaphore_signal(barrier, inc=1, device_id=(lax.rem(tex + o, texels), i, j), device_id_type=MESH)
        return c

    lax.fori_loop(1, PAGES, greet_z, 0)
    lax.fori_loop(1, texels, greet_t, 0)

    own_basis[...] = jnp.zeros_like(own_basis)
    load_basis.wait()
    own_basis[0:VB, 0 : NV * RB] = basis_ref[...]
    load_slab.wait()
    for n in range(2 * NV):
        for l in range(LB):
            dense[n, l * VB : (l + 1) * VB, :] = slab_ref[l, :, n * HB : (n + 1) * HB]

    pl.semaphore_wait(barrier, PAGES - 1 + texels - 1)

    others = [lax.rem(j + o, NV) for o in range(NV)]
    shares = [share_of(i, other) for other in others]

    def rows_of(source):
        return pl.ds(pl.multiple_of(source * ROWS, 16), ROWS)

    def piece_of(p):
        return pl.ds(pl.multiple_of(p * PIECE, 16), PIECE)

    def slab_copy(h, o, slot):
        return remote(
            dense.at[2 * shares[o] + h], share.at[h, rows_of(slot), :], slab_send.at[h, o], slab_recv.at[h, slot],
            (tex, i, others[o]),
        )

    def basis_copy(o, slot):
        return remote(own_basis, all_basis.at[slot], basis_send.at[o], basis_recv.at[slot], (tex, i, others[o]))

    for o in (2, 3, 1):
        basis_copy(o, j).start()
    local = []
    for h in range(2):
        for o in (2, 3, 1):
            slab_copy(h, o, j).start()
        local.append(
            pltpu.make_async_copy(dense.at[2 * mine + h], share.at[h, rows_of(j), :], slab_recv.at[h, j])
        )
        local[-1].start()
    all_basis[j] = own_basis[...]
    for o in (1, 2, 3):
        basis_copy(o, others[o]).wait_recv()

    table = lax.dot_general(
        all_basis[...].reshape(NV * 32, 128), expand_table(), (((0,), (0,)), ((), ())), preferred_element_type=F32
    ).astype(BF)
    mask_ref[...] = light_mask()

    def weight_rows(g, c):
        at = pl.ds(pl.multiple_of(g * GROUP, 16), GROUP)
        full = jnp.dot(spread_rows(g), table, preferred_element_type=F32)
        weights[at, :] = full.astype(BF) * mask_ref[...]
        return c

    lax.fori_loop(0, NV * PIECE // GROUP, weight_rows, 0)

    def light_copy(h, o, ci, cj):
        return remote(
            pieces.at[h, piece_of(others[o]), :], light_land.at[h, i], light_send.at[h, o], light_recv.at[h, i],
            (tex, ci, cj),
        )

    def core_copy(h, o, slot, place):
        return remote(
            pieces.at[h, piece_of(others[o]), :], core_land.at[2 * place + h], core_send.at[h, o],
            core_recv.at[h, slot], (tex, i, others[o]),
        )

    centers = [center_of(mine, p) for p in others]
    for h in range(2):
        local[h].wait()
        for o in (1, 2, 3):
            slab_copy(h, o, others[o]).wait_recv()
        for o in (2, 3, 1, 0):
            at = piece_of(others[o])
            pieces[h, at, :] = jnp.dot(weights[at, :], share[h], preferred_element_type=F32).astype(BF)
            ci, cj = centers[o]
            here = jnp.logical_and(ci == i, cj == j)

            @pl.when(here)
            def _():
                pltpu.make_async_copy(pieces.at[h, at, :], light_land.at[h, i], light_recv.at[h, i]).start()

            @pl.when(jnp.logical_not(here))
            def _():
                light_copy(h, o, ci, cj).start()

    def products(stacks):
        total = None
        for stack in stacks:
            term = lax.dot_general(stack, stack, (((1,), (1,)), ((), ())), preferred_element_type=F32)
            total = term if total is None else total + term
        return total

    def to_pages(total, turned):
        rows = split_dot(pick_table(turned), jnp.where(keep_table(), total, 0.0))
        return split_dot(rows, gather_table()).reshape(PAGES, 8, 128)

    def z_copy(g, o, slot):
        other = lax.rem(me + o, PAGES)
        return remote(
            pages.at[g, other], z_land.at[g, slot(other)], z_send.at[g, o], z_recv.at[g, slot(other)],
            (tex, lax.div(other, NV), lax.rem(other, NV)),
        )

    def t_copy(g, o, slot):
        x, y = lax.div(tex, 4), lax.rem(tex, 4)
        other = 4 * lax.rem(x + o // 4, 4) + lax.rem(y + o % 4, 4)
        return remote(
            part.at[g], t_land.at[g, slot(other)], t_send.at[g, o], t_recv.at[g, slot(other)], (other, i, j)
        )

    def last_copy(g, o, slot):
        other = lax.rem((i, j)[g] + o, 4)
        device = (tex, other, j) if g == 0 else (tex, i, other)
        return remote(
            whole.at[g], last_land.at[g, slot(other)], last_send.at[g, o], last_recv.at[g, slot(other)], device
        )

    def start_all(copy, g, order, own):
        for o in order:
            copy(g, o, lambda other: own).start()

    def wait_all(copy, g, order):
        for o in order:
            copy(g, o, lambda other: other).wait_recv()

    z_order = (8, 7, 9, 6, 10, 5, 11, 4, 12, 3, 13, 2, 14, 1, 15)
    t_order = (10, 9, 11, 6, 14, 8, 2, 5, 7, 13, 15, 4, 12, 1, 3)

    def z_start(g, total):
        pages[g] = to_pages(total, g == 0)
        start_all(z_copy, g, z_order, me)
        z_land[g, me] = pages[g, me]

    def z_end_t_start(g):
        wait_all(z_copy, g, z_order)
        part[g] = jnp.sum(z_land[g], axis=0)
        start_all(t_copy, g, t_order, tex)
        t_land[g, tex] = part[g]

    def t_end_last_start(g):
        wait_all(t_copy, g, t_order)
        whole[g] = jnp.sum(t_land[g], axis=0)
        start_all(last_copy, g, (2, 1, 3), (i, j)[g])
        last_land[g, (i, j)[g]] = whole[g]

    def last_end(g, out, scale):
        wait_all(last_copy, g, (2, 1, 3))
        for q in range(4):
            out[5 * q : 5 * q + 5, :] = last_land[g, q, 0:5, 0:80] * scale

    z_start(0, products(
        jnp.concatenate([share[h, s * ROWS + g * GROUP : s * ROWS + (g + 1) * GROUP, :] for s in range(NV)], axis=0)
        for h in range(2)
        for g in range(ROWS // GROUP)
    ))

    for h in range(2):
        for o in (2, 3, 1):
            core_copy(h, o, j, mine).start()
        pltpu.make_async_copy(
            pieces.at[h, piece_of(j), :], core_land.at[2 * mine + h], core_recv.at[h, j]
        ).start()

    def light_products(h):
        for k in range(NL):
            pltpu.make_async_copy(pieces.at[h, pl.ds(0, PIECE), :], light_land.at[h, k], light_recv.at[h, k]).wait()
        return products(
            jnp.concatenate([light_land[h, k, g * GROUP : (g + 1) * GROUP, :] for k in range(NL)], axis=0)
            for g in range(PIECE // GROUP)
        )

    first = light_products(0)
    z_end_t_start(0)
    z_start(1, first + light_products(1))
    t_end_last_start(0)
    z_end_t_start(1)
    for h in range(2):
        pltpu.make_async_copy(
            pieces.at[h, piece_of(j), :], core_land.at[2 * mine + h], core_recv.at[h, j]
        ).wait()
        for o in (1, 2, 3):
            core_copy(h, o, others[o], shares[o]).wait_recv()
    for n in range(2 * NV):
        core_ref[:, n * HB : (n + 1) * HB] = core_land[n]
    last_end(0, view_ref, view_scale)
    t_end_last_start(1)
    last_end(1, light_ref, light_scale)

    for o in (1, 2, 3):
        basis_copy(o, j).wait_send()
        for h in range(2):
            slab_copy(h, o, j).wait_send()
            core_copy(h, o, j, mine).wait_send()
    for o in range(NV):
        ci, cj = centers[o]

        @pl.when(jnp.logical_not(jnp.logical_and(ci == i, cj == j)))
        def _():
            for h in range(2):
                light_copy(h, o, ci, cj).wait_send()

    for g in range(2):
        for o in z_order:
            z_copy(g, o, lambda other: me).wait_send()
        for o in t_order:
            t_copy(g, o, lambda other: tex).wait_send()
        for o in (2, 1, 3):
            last_copy(g, o, lambda other: (i, j)[g]).wait_send()


def body(slab, basis):
    texels = lax.axis_size("texel")
    columns_all = slab.shape[2] * texels
    view_scale = 1.0 / (LB * NL * columns_all)
    light_scale = 1.0 / (RB * NV * columns_all)
    hbm = pl.BlockSpec(memory_space=pltpu.HBM)
    vmem = pl.BlockSpec(memory_space=pltpu.VMEM)
    dma = pltpu.SemaphoreType.DMA
    view_gram, core, light_gram = pl.pallas_call(
        functools.partial(kernel, view_scale, light_scale),
        out_shape=(
            pltpu.VMEM((VB, 80), F32),
            pltpu.VMEM((PIECE, 4 * CB), BF),
            pltpu.VMEM((LB, 80), F32),
        ),
        in_specs=[hbm] * 2,
        out_specs=(vmem,) * 3,
        scratch_shapes=[
            pltpu.VMEM(slab.shape, BF),
            pltpu.VMEM(basis.shape, BF),
            pltpu.VMEM((GROUP, NV * ROWS), BF),
            pltpu.VMEM((2 * NV, ROWS, HB), BF),
            pltpu.VMEM((2, NV * ROWS, HB), BF),
            pltpu.VMEM((32, 128), BF),
            pltpu.VMEM((NV, 32, 128), BF),
            pltpu.VMEM((NV * PIECE, NV * ROWS), BF),
            pltpu.VMEM((2, NV * PIECE, HB), BF),
            pltpu.VMEM((2 * NV, PIECE, HB), BF),
            pltpu.VMEM((2, NL, PIECE, HB), BF),
            pltpu.VMEM((2, PAGES, 8, 128), F32),
            pltpu.VMEM((2, PAGES, 8, 128), F32),
            pltpu.VMEM((2, 8, 128), F32),
            pltpu.VMEM((2, texels, 8, 128), F32),
            pltpu.VMEM((2, 8, 128), F32),
            pltpu.VMEM((2, 4, 8, 128), F32),
            dma((2,)), dma((NV,)), dma((NV,)), dma((2, NV)), dma((2, NV)), dma((2, NV)), dma((2, NV)),
            dma((2, NV)), dma((2, NL)), dma((2, PAGES)), dma((2, PAGES)), dma((2, texels)), dma((2, texels)),
            dma((2, 4)), dma((2, 4)),
        ],
        compiler_params=pltpu.CompilerParams(
            collective_id=0, has_side_effects=True, vmem_limit_bytes=40 * 1024 * 1024
        ),
    )(pltpu.with_memory_space_constraint(slab, pltpu.HBM), pltpu.with_memory_space_constraint(basis, pltpu.HBM))
    return view_gram, core.reshape(RB, LB, 4 * CB), light_gram


def solution(mesh):
    return jax.shard_map(
        body,
        mesh=mesh,
        in_specs=(P("light", "view", "texel"), P("view", None)),
        out_specs=(P("view", None), P("view", "light", "texel"), P("light", None)),
        check_vma=False,
    )
```

time: 788 us -> 52.9 us (0.07)
  blocking collectives: 648 us -> 0 us
  waiting for transfers between devices: 101 us -> 0 us
  Pallas kernels: 0 us -> 50 us
  between operations: 13.8 us -> 0.64 us
  matrix products: 11.8 us -> 0 us
    psum x2 -> x0, blocking collectives: 648 us -> none  [the longest x1 326 us: row_total(): return lax.psum(partial_value, ('texel', 'light'))]
    reduce_scatter x1 -> x0, waiting for transfers between devices: 53.8 us -> none  [body(): lax.psum_scatter(jnp.einsum('vr,lvc->rlc', basis, slab, preferred_element...]
    pallas_call x0 -> x1, Pallas kernels: none -> 50 us  [body(): pl.pallas_call(functools.partial(kernel, view_scale, light_scale), out_sh...]
    all_gather x2 -> x0, waiting for transfers between devices: 46.8 us -> none  [the longest x1 46.8 us: body(): lax.all_gather(slab, 'view', axis=1, tiled=True)]
    dot_general x3 -> x0, matrix products: 11.8 us -> none  [the longest x1 5.85 us: body(): jnp.einsum('lvc,lwc->vw', slab, lax.all_gather(slab, 'view', axis=1, tile...]
  transfers between devices with their start and end apart: 3 -> 0, of which waited for: 2 -> 0; matrix products, arithmetic and copies ran while one was open for 1% -> 0% of each run, Pallas kernels for 0% -> 0%
where the time goes in v2:
time: 52.9 us; the launch traced here: 52.8 us
  Pallas kernels  50 us (95%)
  local copies, waits for them, and re-layouts  2.11 us (4%)
  between operations  0.64 us (1%)
    pallas_call x1, Pallas kernels, body(): pl.pallas_call(functools.partial(kernel, view_scale, light_scale), out_sh...  50 us
    unnamed x2, local copies, waits for them, and re-layouts  1.2 us

profile of v2, /device:TPU:1, one launch (start us, length us, event | category | flops | bytes accessed | tf_op | source)
XLA Modules:
  0.0 52.8 jit_solution(16907090725458371588)
XLA Ops:
  0.6 50.0 %shard_map.49 = (f32[20,80]{1,0:T(8,128)S(1)}, bf16[240,1024]{1,0:T(8,128)(2,1)S(1)}, f32[20,80]{1,0:T(8,128)S(1)}) custom-call(bf16[20,20,1024]{2,1,0:T(8,128)(2,1)} %slab_hbm.1, bf16[20,48]{1,0:T(8,128)(2,1)} %basis_hbm.1), custom_call_target="tpu_custom_call" | custom-call | tf_op jit(solution)/shard_map/pallas_call | solution.py:369
  50.7 0.6 %copy.7 = f32[20,80]{1,0:T(8,128)} copy(f32[20,80]{1,0:T(8,128)S(1)} %get-tuple-element.9) | data formatting | bytes 12800
  51.3 0.6 %copy.8 = f32[20,80]{1,0:T(8,128)} copy(f32[20,80]{1,0:T(8,128)S(1)} %get-tuple-element.11) | data formatting | bytes 12800
  51.9 0.9 %reshape.9 = bf16[12,20,1024]{2,1,0:T(8,128)(2,1)} reshape(bf16[240,1024]{1,0:T(8,128)(2,1)S(1)} %get-tuple-element.7) | data formatting | bytes 983040 | tf_op jit(solution)/shard_map/reshape | solution.py:404

commit v3 on v2

v3 whole, which is shorter than its diff:
```python
import jax
import jax.numpy as jnp
from jax import lax
from jax.experimental import pallas as pl
from jax.experimental.pallas import tpu as pltpu
from jax.sharding import PartitionSpec as P

MESH = pl.DeviceIdType.MESH
BF = jnp.bfloat16
F32 = jnp.float32
LB = 20
VB = 20
NV = 4
NL = 4
RB = 12
CB = 256
ROWS = LB * VB
PIECE = RB * LB
NG = 5
GROUP = 4 * VB
STACK = NV * GROUP
AHEAD = 3
PART = 4 * RB
PAGES = NL * NV


def cells(shape):
    return lax.broadcasted_iota(jnp.int32, shape, 0), lax.broadcasted_iota(jnp.int32, shape, 1)


def div20(x):
    return (x * 3277) >> 16


def ones_where(condition, dtype=BF):
    return jnp.where(condition, 1.0, 0.0).astype(dtype)


def expand_table():
    row, col = cells((NV * 32, STACK))
    line = div20(col)
    return ones_where(row == 32 * (line >> 2) + col - VB * line)


def spread_table():
    row, col = cells((NV * PART, 128))
    return ones_where((row >> 2) == col)


def light_mask():
    row, col = cells((NV * PART, STACK))
    return ones_where((row & 3) == (div20(col) & 3))


def order_table():
    row, col = cells((PIECE, PIECE))
    group = (col * 1366) >> 16
    rest = col - PART * group
    return ones_where(row == LB * (rest >> 2) + 4 * group + (rest & 3))


def gram_place(g, x):
    if g:
        return 4 * (x >> 4) + (x & 3), (x >> 2) & 3
    line = div20(x)
    return 20 * (line >> 2) + x - 20 * line, line & 3


def keep_table(g):
    row, col = cells((STACK, STACK))
    return ones_where(gram_place(g, row)[1] == gram_place(g, col)[1], F32)


def pick_table(g):
    row, col = cells((8 * PAGES, STACK))
    p, q = row >> 3, row & 7
    if g == 0:
        p = NL * (p & 3) + (p >> 2)
    return ones_where((q < 5) & (5 * p + q == gram_place(g, col)[0]))


def gather_table(g):
    row, col = cells((STACK, 128))
    return ones_where(gram_place(g, row)[0] == col)


def odd_share(k, t):
    return lax.rem(lax.div(k + 1 - t, 2), 2)


def share_of(k, j):
    e, t = lax.div(j, 2), lax.rem(j, 2)
    return 2 * t + lax.rem(odd_share(k, t) + 1 - e, 2)


def member_for(k, b):
    t, u = lax.div(b, 2), lax.rem(b, 2)
    return 2 * lax.rem(odd_share(k, t) + 1 + u, 2) + t


def center_of(b, n):
    t, u = lax.div(b, 2), lax.rem(b, 2)
    z = lax.rem(1 + 4 * u + 2 * t + lax.div(n, 2), 8)
    return lax.div(z, 2), 2 * lax.rem(z, 2) + lax.rem(n, 2)


def split_dot(a, b):
    def parts(x):
        hi = x.astype(BF)
        return hi, (x - hi.astype(F32)).astype(BF)

    if a.dtype == BF:
        return sum(jnp.dot(a, p, preferred_element_type=F32) for p in parts(b))
    return sum(jnp.dot(p, b, preferred_element_type=F32) for p in parts(a))


def remote(src, dst, send, recv, device):
    return pltpu.make_async_remote_copy(
        src_ref=src, dst_ref=dst, send_sem=send, recv_sem=recv, device_id=device, device_id_type=MESH
    )


def kernel(
    slab_hbm, basis_hbm,
    gram_ref, core_ref,
    slab_ref, basis_ref, keep_ref, pick_ref, gather_ref, order_ref, weights,
    dense, share, own_basis, all_basis, pieces, core_land, light_land,
    pages, z_land, part, t_land, whole, last_land,
    load, basis_send, basis_recv, slab_send, slab_recv, core_send, core_recv,
    light_send, light_recv, z_send, z_recv, t_send, t_recv, last_send, last_recv,
):
    texels = lax.axis_size("texel")
    tex, i, j = lax.axis_index("texel"), lax.axis_index("light"), lax.axis_index("view")
    me = i * NV + j
    mine = share_of(i, j)

    load_basis = pltpu.make_async_copy(basis_hbm, basis_ref, load.at[NG])
    load_basis.start()
    load_slab = [
        pltpu.make_async_copy(slab_hbm.at[4 * g : 4 * g + 4], slab_ref.at[4 * g : 4 * g + 4], load.at[g])
        for g in range(NG)
    ]
    for copy in load_slab:
        copy.start()
    barrier = pltpu.get_barrier_semaphore()

    def greet_z(o, c):
        other = lax.rem(me + o, PAGES)
        pl.semaphore_signal(
            barrier, inc=1, device_id=(tex, lax.div(other, NV), lax.rem(other, NV)), device_id_type=MESH
        )
        return c

    def greet_t(o, c):
        pl.semaphore_signal(barrier, inc=1, device_id=(lax.rem(tex + o, texels), i, j), device_id_type=MESH)
        return c

    lax.fori_loop(1, PAGES, greet_z, 0)
    lax.fori_loop(1, texels, greet_t, 0)

    own_basis[...] = jnp.zeros_like(own_basis)
    load_basis.wait()
    own_basis[0:VB, 0 : NV * RB] = basis_ref[...]

    def lay_out(g):
        load_slab[g].wait()
        for n in range(NV):
            for l in range(4 * g, 4 * g + 4):
                dense[n, l * VB : (l + 1) * VB, :] = slab_ref[l, :, n * CB : (n + 1) * CB]

    lay_out(0)
    pl.semaphore_wait(barrier, PAGES - 1 + texels - 1)

    others = [lax.rem(j + o, NV) for o in range(NV)]
    shares = [share_of(i, other) for other in others]

    def rows_of(g):
        return pl.ds(g * GROUP, GROUP)

    def part_of(p):
        return pl.ds(pl.multiple_of(p * PART, 16), PART)

    def slab_copy(g, o, slot):
        return remote(
            dense.at[shares[o], rows_of(g), :], share.at[slot, rows_of(g), :], slab_send.at[g, o],
            slab_recv.at[g, slot], (tex, i, others[o]),
        )

    def basis_copy(o, slot):
        return remote(own_basis, all_basis.at[slot], basis_send.at[o], basis_recv.at[slot], (tex, i, others[o]))

    for o in (2, 3, 1):
        basis_copy(o, j).start()
    local = [
        pltpu.make_async_copy(dense.at[mine, rows_of(g), :], share.at[j, rows_of(g), :], slab_recv.at[g, j])
        for g in range(NG)
    ]

    def slab_start(g):
        for o in (2, 3, 1):
            slab_copy(g, o, j).start()
        local[g].start()

    for g in range(NG):
        if g:
            lay_out(g)
        if g < AHEAD:
            slab_start(g)
    all_basis[j] = own_basis[...]
    spread, expand, mask = spread_table(), expand_table(), light_mask()
    for o in (1, 2, 3):
        basis_copy(o, others[o]).wait_recv()

    table = lax.dot_general(
        all_basis[...].reshape(NV * 32, 128), expand, (((0,), (0,)), ((), ())), preferred_element_type=F32
    ).astype(BF)
    weights[...] = jnp.dot(spread, table, preferred_element_type=F32).astype(BF) * mask

    ahead = lax.rem(1 + 4 * lax.rem(mine, 2) + 2 * lax.div(mine, 2) - 2 * i - lax.div(j, 2) + 8, 8)
    far = 1 - lax.div(ahead, 4)
    turns = [2 * far, 2 * far + 1, 2 * (1 - far), 2 * (1 - far) + 1]
    centers = [center_of(mine, p) for p in turns]

    def light_copy(g, o, ci, cj):
        return remote(
            pieces.at[g, part_of(turns[o]), :], light_land.at[i, g], light_send.at[g, o], light_recv.at[g, i],
            (tex, ci, cj),
        )

    def core_copy(o, slot, place):
        return remote(
            pieces.at[:, part_of(others[o]), :], core_land.at[place], core_send.at[o], core_recv.at[slot],
            (tex, i, others[o]),
        )

    def stack_of(g):
        return jnp.concatenate([share[s, g * GROUP : (g + 1) * GROUP, :] for s in range(NV)], axis=0)

    for g in range(NG):
        local[g].wait()
        for o in (1, 2, 3):
            slab_copy(g, o, others[o]).wait_recv()
        if g + AHEAD < NG:
            slab_start(g + AHEAD)
        pieces[g] = jnp.dot(weights[...], stack_of(g), preferred_element_type=F32).astype(BF)
        for o in range(NV):
            ci, cj = centers[o]
            here = jnp.logical_and(ci == i, cj == j)

            @pl.when(here)
            def _():
                pltpu.make_async_copy(
                    pieces.at[g, part_of(turns[o]), :], light_land.at[i, g], light_recv.at[g, i]
                ).start()

            @pl.when(jnp.logical_not(here))
            def _():
                light_copy(g, o, ci, cj).start()

    def products(stacks):
        wide = jnp.concatenate(list(stacks), axis=1)
        return lax.dot_general(wide, wide, (((1,), (1,)), ((), ())), preferred_element_type=F32)

    def to_pages(g, total):
        rows = split_dot(pick_ref[g], total * keep_ref[g])
        return split_dot(rows, gather_ref[g]).reshape(PAGES, 8, 128)

    def z_copy(g, o, slot):
        other = lax.rem(me + o, PAGES)
        return remote(
            pages.at[g, other], z_land.at[g, slot(other)], z_send.at[g, o], z_recv.at[g, slot(other)],
            (tex, lax.div(other, NV), lax.rem(other, NV)),
        )

    def t_copy(g, o, slot):
        x, y = lax.div(tex, 4), lax.rem(tex, 4)
        other = 4 * lax.rem(x + o // 4, 4) + lax.rem(y + o % 4, 4)
        return remote(
            part.at[g], t_land.at[g, slot(other)], t_send.at[g, o], t_recv.at[g, slot(other)], (other, i, j)
        )

    def last_copy(g, o, slot):
        other = lax.rem((i, j)[g] + o, 4)
        device = (tex, other, j) if g == 0 else (tex, i, other)
        return remote(
            whole.at[g], last_land.at[g, slot(other)], last_send.at[g, o], last_recv.at[g, slot(other)], device
        )

    def start_all(copy, g, order, own):
        for o in order:
            copy(g, o, lambda other: own).start()

    def wait_all(copy, g, order):
        for o in order:
            copy(g, o, lambda other: other).wait_recv()

    z_order = (8, 7, 9, 6, 10, 5, 11, 4, 12, 3, 13, 2, 14, 1, 15)
    t_order = (10, 9, 11, 6, 14, 8, 2, 5, 7, 13, 15, 4, 12, 1, 3)

    def z_start(g, total):
        pages[g] = to_pages(g, total)
        start_all(z_copy, g, z_order, me)
        z_land[g, me] = pages[g, me]

    def z_end_t_start(g):
        wait_all(z_copy, g, z_order)
        part[g] = jnp.sum(z_land[g], axis=0)
        start_all(t_copy, g, t_order, tex)
        t_land[g, tex] = part[g]

    def t_end_last_start(g):
        wait_all(t_copy, g, t_order)
        whole[g] = jnp.sum(t_land[g], axis=0)
        start_all(last_copy, g, (2, 1, 3), (i, j)[g])
        last_land[g, (i, j)[g]] = whole[g]

    def last_end(g):
        wait_all(last_copy, g, (2, 1, 3))
        for q in range(4):
            gram_ref[g, 5 * q : 5 * q + 5, :] = last_land[g, q, 0:5, 0:80]

    for g in range(2):
        keep_ref[g] = keep_table(g)
        pick_ref[g] = pick_table(g)
        gather_ref[g] = gather_table(g)
    z_start(0, products(stack_of(g) for g in range(NG)))

    for o in (2, 3, 1):
        core_copy(o, j, mine).start()
    own_piece = pltpu.make_async_copy(pieces.at[:, part_of(j), :], core_land.at[mine], core_recv.at[j])
    own_piece.start()
    order_ref[...] = order_table()

    for g in range(NG):
        for k in range(NL):
            pltpu.make_async_copy(pieces.at[g, part_of(0), :], light_land.at[k, g], light_recv.at[g, k]).wait()
    z_start(1, products(
        jnp.concatenate(
            [light_land[k, g, 16 * m : 16 * m + 16, :] for k in range(NL) for g in range(NG)], axis=0
        )
        for m in range(PART // 16)
    ))
    z_end_t_start(0)
    for o in (1, 2, 3):
        basis_copy(o, j).wait_send()
        for g in range(NG):
            slab_copy(g, o, j).wait_send()
    for o in range(NV):
        ci, cj = centers[o]

        @pl.when(jnp.logical_not(jnp.logical_and(ci == i, cj == j)))
        def _():
            for g in range(NG):
                light_copy(g, o, ci, cj).wait_send()

    z_end_t_start(1)
    t_end_last_start(0)
    own_piece.wait()
    for o in (1, 2, 3):
        core_copy(o, others[o], shares[o]).wait_recv()
    for n in range(NV):
        core_ref[:, n * CB : (n + 1) * CB] = jnp.dot(
            order_ref[...], core_land[n].reshape(PIECE, CB), preferred_element_type=F32
        ).astype(BF)
    for o in (1, 2, 3):
        core_copy(o, j, mine).wait_send()
    for o in t_order:
        t_copy(0, o, lambda other: tex).wait_send()
    for g in range(2):
        for o in z_order:
            z_copy(g, o, lambda other: me).wait_send()
    t_end_last_start(1)
    for o in t_order:
        t_copy(1, o, lambda other: tex).wait_send()
    last_end(0)
    last_end(1)

    for g in range(2):
        for o in (2, 1, 3):
            last_copy(g, o, lambda other: (i, j)[g]).wait_send()


def body(slab, basis):
    texels = lax.axis_size("texel")
    columns_all = slab.shape[2] * texels
    view_scale = 1.0 / (LB * NL * columns_all)
    light_scale = 1.0 / (RB * NV * columns_all)
    hbm = pl.BlockSpec(memory_space=pltpu.HBM)
    vmem = pl.BlockSpec(memory_space=pltpu.VMEM)
    dma = pltpu.SemaphoreType.DMA
    grams, core = pl.pallas_call(
        kernel,
        out_shape=(
            pltpu.VMEM((2, VB, 80), F32),
            pltpu.VMEM((PIECE, 4 * CB), BF),
        ),
        in_specs=[hbm] * 2,
        out_specs=(vmem,) * 2,
        scratch_shapes=[
            pltpu.VMEM(slab.shape, BF),
            pltpu.VMEM(basis.shape, BF),
            pltpu.VMEM((2, STACK, STACK), F32),
            pltpu.VMEM((2, 8 * PAGES, STACK), BF),
            pltpu.VMEM((2, STACK, 128), BF),
            pltpu.VMEM((PIECE, PIECE), BF),
            pltpu.VMEM((NV * PART, STACK), BF),
            pltpu.VMEM((NV, ROWS, CB), BF),
            pltpu.VMEM((NV, ROWS, CB), BF),
            pltpu.VMEM((32, 128), BF),
            pltpu.VMEM((NV, 32, 128), BF),
            pltpu.VMEM((NG, NV * PART, CB), BF),
            pltpu.VMEM((NV, NG, PART, CB), BF),
            pltpu.VMEM((NL, NG, PART, CB), BF),
            pltpu.VMEM((2, PAGES, 8, 128), F32),
            pltpu.VMEM((2, PAGES, 8, 128), F32),
            pltpu.VMEM((2, 8, 128), F32),
            pltpu.VMEM((2, texels, 8, 128), F32),
            pltpu.VMEM((2, 8, 128), F32),
            pltpu.VMEM((2, 4, 8, 128), F32),
            dma((NG + 1,)), dma((NV,)), dma((NV,)), dma((NG, NV)), dma((NG, NV)), dma((NV,)), dma((NV,)),
            dma((NG, NV)), dma((NG, NL)), dma((2, PAGES)), dma((2, PAGES)), dma((2, texels)), dma((2, texels)),
            dma((2, 4)), dma((2, 4)),
        ],
        compiler_params=pltpu.CompilerParams(
            collective_id=0, has_side_effects=True, vmem_limit_bytes=40 * 1024 * 1024
        ),
    )(pltpu.with_memory_space_constraint(slab, pltpu.HBM), pltpu.with_memory_space_constraint(basis, pltpu.HBM))
    return grams[0] * view_scale, core.reshape(RB, LB, 4 * CB), grams[1] * light_scale


def solution(mesh):
    return jax.shard_map(
        body,
        mesh=mesh,
        in_specs=(P("light", "view", "texel"), P("view", None)),
        out_specs=(P("view", None), P("view", "light", "texel"), P("light", None)),
        check_vma=False,
    )
```

time: 52.9 us -> 49.5 us (0.936)
  Pallas kernels: 50 us -> 47.3 us
  local copies, waits for them, and re-layouts: 2.11 us -> 0.91 us
  other arithmetic: 0 us -> 0.61 us
    pallas_call x1, Pallas kernels: 50 us -> 47.3 us  [body(): pl.pallas_call(kernel, out_shape=(pltpu.VMEM((2, VB, 80), F32), pltpu.VME...]
    unnamed x2 -> x0, local copies, waits for them, and re-layouts: 1.2 us -> none
    mul x0 -> x1, other arithmetic: none -> 0.61 us  [body(): grams[1] * light_scale]
where the time goes in v3:
time: 49.5 us; the launch traced here: 49.4 us
  Pallas kernels  47.3 us (96%)
  local copies, waits for them, and re-layouts  0.91 us (2%)
  between operations  0.64 us (1%)
  other arithmetic  0.61 us (1%)
    pallas_call x1, Pallas kernels, body(): pl.pallas_call(kernel, out_shape=(pltpu.VMEM((2, VB, 80), F32), pltpu.VME...  47.3 us

profile of v3, /device:TPU:1, one launch (start us, length us, event | category | flops | bytes accessed | tf_op | source)
XLA Modules:
  0.0 49.4 jit_solution(8507840355797811478)
XLA Ops:
  0.6 47.3 %shard_map.49 = (f32[2,20,80]{2,1,0:T(8,128)S(1)}, bf16[240,1024]{1,0:T(8,128)(2,1)S(1)}) custom-call(bf16[20,20,1024]{2,1,0:T(8,128)(2,1)} %slab_hbm.1, bf16[20,48]{1,0:T(8,128)(2,1)} %basis_hbm.1), custom_call_target="tpu_custom_call" | custom-call | tf_op jit(solution)/shard_map/pallas_call | solution.py:391
  47.9 0.6 %multiply_bitcast_fusion = (f32[20,80]{1,0:T(8,128)}, f32[20,80]{1,0:T(8,128)}) fusion(f32[2,20,80]{2,1,0:T(8,128)S(1)} %get-tuple-element.5), kind=kLoop, calls=%fused_computation | loop fusion | flops 3200 | bytes 25600 | tf_op jit(solution)/shard_map/mul | solution.py:428
  48.5 0.9 %reshape.13 = bf16[12,20,1024]{2,1,0:T(8,128)(2,1)} reshape(bf16[240,1024]{1,0:T(8,128)(2,1)S(1)} %get-tuple-element.6) | data formatting | bytes 983040 | tf_op jit(solution)/shard_map/reshape | solution.py:428

commit v4 on v3

--- a/solution.py
+++ b/solution.py
@@ -74,8 +74,6 @@
 def pick_table(g):
     row, col = cells((8 * PAGES, STACK))
     p, q = row >> 3, row & 7
-    if g == 0:
-        p = NL * (p & 3) + (p >> 2)
     return ones_where((q < 5) & (5 * p + q == gram_place(g, col)[0]))
 
 
@@ -127,7 +125,7 @@
     dense, share, own_basis, all_basis, pieces, core_land, light_land,
     pages, z_land, part, t_land, whole, last_land,
     load, basis_send, basis_recv, slab_send, slab_recv, core_send, core_recv,
-    light_send, light_recv, z_send, z_recv, t_send, t_recv, last_send, last_recv,
+    light_send, light_recv, z_send, z_recv, t_send, t_recv, last_send, last_recv, vz_send, vlast_send,
 ):
     texels = lax.axis_size("texel")
     tex, i, j = lax.axis_index("texel"), lax.axis_index("light"), lax.axis_index("view")
@@ -265,65 +263,70 @@
         rows = split_dot(pick_ref[g], total * keep_ref[g])
         return split_dot(rows, gather_ref[g]).reshape(PAGES, 8, 128)
 
-    def z_copy(g, o, slot):
+    x, y = lax.div(tex, 4), lax.rem(tex, 4)
+
+    def texel_at(o):
+        return 4 * lax.rem(x + o // 4, 4) + lax.rem(y + o % 4, 4)
+
+    def z_copy(o, slot):
         other = lax.rem(me + o, PAGES)
         return remote(
-            pages.at[g, other], z_land.at[g, slot(other)], z_send.at[g, o], z_recv.at[g, slot(other)],
+            pages.at[1, other], z_land.at[1, slot(other)], z_send.at[o], z_recv.at[1, slot(other)],
             (tex, lax.div(other, NV), lax.rem(other, NV)),
         )
 
-    def t_copy(g, o, slot):
-        x, y = lax.div(tex, 4), lax.rem(tex, 4)
-        other = 4 * lax.rem(x + o // 4, 4) + lax.rem(y + o % 4, 4)
-        return remote(
-            part.at[g], t_land.at[g, slot(other)], t_send.at[g, o], t_recv.at[g, slot(other)], (other, i, j)
-        )
-
-    def last_copy(g, o, slot):
-        other = lax.rem((i, j)[g] + o, 4)
-        device = (tex, other, j) if g == 0 else (tex, i, other)
-        return remote(
-            whole.at[g], last_land.at[g, slot(other)], last_send.at[g, o], last_recv.at[g, slot(other)], device
-        )
-
-    def start_all(copy, g, order, own):
+    def t_copy(o, slot):
+        other = texel_at(o)
+        return remote(
+            part.at[1], t_land.at[1, slot(other)], t_send.at[1, o], t_recv.at[1, slot(other)], (other, i, j)
+        )
+
+    def last_copy(o, slot):
+        other = lax.rem(j + o, NV)
+        return remote(
+            whole.at[1], last_land.at[1, slot(other)], last_send.at[o], last_recv.at[1, slot(other)], (tex, i, other)
+        )
+
+    takes = j == x
+
+    def vt_copy(o, slot):
+        other = texel_at(o)
+        return remote(
+            pages.at[0, other], t_land.at[0, slot(other)], t_send.at[0, o], t_recv.at[0, slot(other)], (other, i, j)
+        )
+
+    def vz_copy(o, slot):
+        return remote(
+            part.at[0], z_land.at[0, slot], vz_send.at[o], z_recv.at[0, slot], (tex, lax.rem(i + o, NL), x)
+        )
+
+    def vlast_copy(o, slot):
+        return remote(
+            whole.at[0], last_land.at[0, slot], vlast_send.at[o], last_recv.at[0, slot], (texel_at(o), i, j)
+        )
+
+    def start_all(copy, order, own):
         for o in order:
-            copy(g, o, lambda other: own).start()
-
-    def wait_all(copy, g, order):
+            copy(o, lambda other: own).start()
+
+    def wait_all(copy, order):
         for o in order:
-            copy(g, o, lambda other: other).wait_recv()
+            copy(o, lambda other: other).wait_recv()
+
+    def sent_all(copy, order, own):
+        for o in order:
+            copy(o, lambda other: own).wait_send()
 
     z_order = (8, 7, 9, 6, 10, 5, 11, 4, 12, 3, 13, 2, 14, 1, 15)
     t_order = (10, 9, 11, 6, 14, 8, 2, 5, 7, 13, 15, 4, 12, 1, 3)
-
-    def z_start(g, total):
-        pages[g] = to_pages(g, total)
-        start_all(z_copy, g, z_order, me)
-        z_land[g, me] = pages[g, me]
-
-    def z_end_t_start(g):
-        wait_all(z_copy, g, z_order)
-        part[g] = jnp.sum(z_land[g], axis=0)
-        start_all(t_copy, g, t_order, tex)
-        t_land[g, tex] = part[g]
-
-    def t_end_last_start(g):
-        wait_all(t_copy, g, t_order)
-        whole[g] = jnp.sum(t_land[g], axis=0)
-        start_all(last_copy, g, (2, 1, 3), (i, j)[g])
-        last_land[g, (i, j)[g]] = whole[g]
-
-    def last_end(g):
-        wait_all(last_copy, g, (2, 1, 3))
-        for q in range(4):
-            gram_ref[g, 5 * q : 5 * q + 5, :] = last_land[g, q, 0:5, 0:80]
 
     for g in range(2):
         keep_ref[g] = keep_table(g)
         pick_ref[g] = pick_table(g)
         gather_ref[g] = gather_table(g)
-    z_start(0, products(stack_of(g) for g in range(NG)))
+    pages[0] = to_pages(0, products(stack_of(g) for g in range(NG)))
+    start_all(vt_copy, t_order, tex)
+    t_land[0, tex] = pages[0, tex]
 
     for o in (2, 3, 1):
         core_copy(o, j, mine).start()
@@ -334,13 +337,28 @@
     for g in range(NG):
         for k in range(NL):
             pltpu.make_async_copy(pieces.at[g, part_of(0), :], light_land.at[k, g], light_recv.at[g, k]).wait()
-    z_start(1, products(
+    pages[1] = to_pages(1, products(
         jnp.concatenate(
             [light_land[k, g, 16 * m : 16 * m + 16, :] for k in range(NL) for g in range(NG)], axis=0
         )
         for m in range(PART // 16)
     ))
-    z_end_t_start(0)
+    start_all(z_copy, z_order, me)
+    z_land[1, me] = pages[1, me]
+
+    wait_all(vt_copy, t_order)
+    part[0] = jnp.sum(t_land[0], axis=0)
+    for o in (2, 1, 3):
+        vz_copy(o, me).start()
+
+    @pl.when(takes)
+    def _():
+        z_land[0, me] = part[0]
+
+    @pl.when(jnp.logical_not(takes))
+    def _():
+        vz_copy(0, me).start()
+
     for o in (1, 2, 3):
         basis_copy(o, j).wait_send()
         for g in range(NG):
@@ -353,8 +371,21 @@
             for g in range(NG):
                 light_copy(g, o, ci, cj).wait_send()
 
-    z_end_t_start(1)
-    t_end_last_start(0)
+    sent_all(vt_copy, t_order, tex)
+    wait_all(z_copy, z_order)
+    part[1] = jnp.sum(z_land[1], axis=0)
+    start_all(t_copy, t_order, tex)
+    t_land[1, tex] = part[1]
+
+    @pl.when(takes)
+    def _():
+        for o in z_order:
+            vz_copy(0, lax.rem(me + o, PAGES)).wait_recv()
+        whole[0] = jnp.sum(z_land[0], axis=0)
+        for o in t_order:
+            vlast_copy(o, y).start()
+        last_land[0, y] = whole[0]
+
     own_piece.wait()
     for o in (1, 2, 3):
         core_copy(o, others[o], shares[o]).wait_recv()
@@ -364,20 +395,34 @@
         ).astype(BF)
     for o in (1, 2, 3):
         core_copy(o, j, mine).wait_send()
-    for o in t_order:
-        t_copy(0, o, lambda other: tex).wait_send()
+        vz_copy(o, me).wait_send()
+
+    @pl.when(jnp.logical_not(takes))
+    def _():
+        vz_copy(0, me).wait_send()
+
+    sent_all(z_copy, z_order, me)
+    wait_all(t_copy, t_order)
+    whole[1] = jnp.sum(t_land[1], axis=0)
+    start_all(last_copy, (2, 1, 3), j)
+    last_land[1, j] = whole[1]
+
+    for q in range(4):
+        @pl.when(jnp.logical_not(jnp.logical_and(takes, y == q)))
+        def _():
+            vlast_copy(1, q).wait_recv()
+
+    @pl.when(takes)
+    def _():
+        for o in t_order:
+            vlast_copy(o, y).wait_send()
+
+    sent_all(t_copy, t_order, tex)
+    wait_all(last_copy, (2, 1, 3))
     for g in range(2):
-        for o in z_order:
-            z_copy(g, o, lambda other: me).wait_send()
-    t_end_last_start(1)
-    for o in t_order:
-        t_copy(1, o, lambda other: tex).wait_send()
-    last_end(0)
-    last_end(1)
-
-    for g in range(2):
-        for o in (2, 1, 3):
-            last_copy(g, o, lambda other: (i, j)[g]).wait_send()
+        for q in range(4):
+            gram_ref[g, 5 * q : 5 * q + 5, :] = last_land[g, q, 0:5, 0:80]
+    sent_all(last_copy, (2, 1, 3), j)
 
 
 def body(slab, basis):
@@ -418,8 +463,8 @@
             pltpu.VMEM((2, 8, 128), F32),
             pltpu.VMEM((2, 4, 8, 128), F32),
             dma((NG + 1,)), dma((NV,)), dma((NV,)), dma((NG, NV)), dma((NG, NV)), dma((NV,)), dma((NV,)),
-            dma((NG, NV)), dma((NG, NL)), dma((2, PAGES)), dma((2, PAGES)), dma((2, texels)), dma((2, texels)),
-            dma((2, 4)), dma((2, 4)),
+            dma((NG, NV)), dma((NG, NL)), dma((PAGES,)), dma((2, PAGES)), dma((2, texels)), dma((2, texels)),
+            dma((4,)), dma((2, 4)), dma((NL,)), dma((texels,)),
         ],
         compiler_params=pltpu.CompilerParams(
             collective_id=0, has_side_effects=True, vmem_limit_bytes=40 * 1024 * 1024

time: 49.5 us -> 48.2 us (0.974)
  Pallas kernels: 47.3 us -> 45.9 us
    pallas_call x1, Pallas kernels: 47.3 us -> 45.9 us  [body(): pl.pallas_call(kernel, out_shape=(pltpu.VMEM((2, VB, 80), F32), pltpu.VME...]
where the time goes in v4:
time: 48.2 us; the launch traced here: 48.1 us
  Pallas kernels  45.9 us (95%)
  local copies, waits for them, and re-layouts  0.91 us (2%)
  between operations  0.64 us (1%)
  other arithmetic  0.61 us (1%)
    pallas_call x1, Pallas kernels, body(): pl.pallas_call(kernel, out_shape=(pltpu.VMEM((2, VB, 80), F32), pltpu.VME...  45.9 us

profile of v4, /device:TPU:1, one launch (start us, length us, event | category | flops | bytes accessed | tf_op | source)
XLA Modules:
  0.0 48.1 jit_solution(13456465444963121734)
XLA Ops:
  0.6 45.9 %shard_map.49 = (f32[2,20,80]{2,1,0:T(8,128)S(1)}, bf16[240,1024]{1,0:T(8,128)(2,1)S(1)}) custom-call(bf16[20,20,1024]{2,1,0:T(8,128)(2,1)} %slab_hbm.1, bf16[20,48]{1,0:T(8,128)(2,1)} %basis_hbm.1), custom_call_target="tpu_custom_call" | custom-call | tf_op jit(solution)/shard_map/pallas_call | solution.py:436
  46.5 0.6 %multiply_bitcast_fusion = (f32[20,80]{1,0:T(8,128)}, f32[20,80]{1,0:T(8,128)}) fusion(f32[2,20,80]{2,1,0:T(8,128)S(1)} %get-tuple-element.5), kind=kLoop, calls=%fused_computation | loop fusion | flops 3200 | bytes 25600 | tf_op jit(solution)/shard_map/mul | solution.py:473
  47.1 0.9 %reshape.13 = bf16[12,20,1024]{2,1,0:T(8,128)(2,1)} reshape(bf16[240,1024]{1,0:T(8,128)(2,1)S(1)} %get-tuple-element.6) | data formatting | bytes 983040 | tf_op jit(solution)/shard_map/reshape | solution.py:473

commit v5 on v4

--- a/solution.py
+++ b/solution.py
@@ -82,6 +82,21 @@
     return ones_where(gram_place(g, row)[0] == col)
 
 
+def packed_tables():
+    row, col = cells((3 * 64, STACK))
+    piece, p, q = row >> 6, (row >> 3) & 7, row & 7
+    wanted = 10 * p + jnp.where(piece == 0, q, 8 + (q >> 1))
+    here = (piece == 0) | ((q < 4) & ((q & 1) == piece - 1))
+    pick = ones_where(here & (wanted == gram_place(1, col)[0]))
+    row, col = cells((3 * STACK, 128))
+    piece = jnp.where(row >= STACK, 1, 0) + jnp.where(row >= 2 * STACK, 1, 0)
+    column = gram_place(1, row - STACK * piece)[0]
+    place = jnp.where(piece == 0, column, column + 120 - 40 * piece)
+    low = 40 * jnp.maximum(piece - 1, 0)
+    fits = (piece == 0) | ((column >= low) & (column < low + 40))
+    return pick, ones_where(fits & (place == col))
+
+
 def odd_share(k, t):
     return lax.rem(lax.div(k + 1 - t, 2), 2)
 
@@ -121,9 +136,9 @@
 def kernel(
     slab_hbm, basis_hbm,
     gram_ref, core_ref,
-    slab_ref, basis_ref, keep_ref, pick_ref, gather_ref, order_ref, weights,
+    slab_ref, basis_ref, keep_ref, pick_ref, gather_ref, packed_pick_ref, packed_gather_ref, order_ref, weights,
     dense, share, own_basis, all_basis, pieces, core_land, light_land,
-    pages, z_land, part, t_land, whole, last_land,
+    pages, light_pages, z_land, part, t_land, whole, last_land,
     load, basis_send, basis_recv, slab_send, slab_recv, core_send, core_recv,
     light_send, light_recv, z_send, z_recv, t_send, t_recv, last_send, last_recv, vz_send, vlast_send,
 ):
@@ -169,7 +184,7 @@
     lay_out(0)
     pl.semaphore_wait(barrier, PAGES - 1 + texels - 1)
 
-    others = [lax.rem(j + o, NV) for o in range(NV)]
+    others = [j, j + 1 - 2 * lax.rem(j, 2), lax.rem(j + 2, NV), NV - 1 - j]
     shares = [share_of(i, other) for other in others]
 
     def rows_of(g):
@@ -259,20 +274,30 @@
         wide = jnp.concatenate(list(stacks), axis=1)
         return lax.dot_general(wide, wide, (((1,), (1,)), ((), ())), preferred_element_type=F32)
 
-    def to_pages(g, total):
-        rows = split_dot(pick_ref[g], total * keep_ref[g])
-        return split_dot(rows, gather_ref[g]).reshape(PAGES, 8, 128)
+    def to_pages(total):
+        rows = split_dot(pick_ref[...], total * keep_ref[0])
+        return split_dot(rows, gather_ref[...]).reshape(PAGES, 8, 128)
+
+    def to_packed(total):
+        rows = split_dot(packed_pick_ref[...], total * keep_ref[1])
+        return sum(
+            split_dot(rows[64 * n : 64 * n + 64], packed_gather_ref[STACK * n : STACK * n + STACK, :])
+            for n in range(3)
+        ).reshape(8, 8, 128)
 
     x, y = lax.div(tex, 4), lax.rem(tex, 4)
 
     def texel_at(o):
         return 4 * lax.rem(x + o // 4, 4) + lax.rem(y + o % 4, 4)
 
+    core = lax.rem(j, 2)
+
     def z_copy(o, slot):
         other = lax.rem(me + o, PAGES)
-        return remote(
-            pages.at[1, other], z_land.at[1, slot(other)], z_send.at[o], z_recv.at[1, slot(other)],
-            (tex, lax.div(other, NV), lax.rem(other, NV)),
+        ci, cj = lax.div(other, NV), lax.rem(other, NV)
+        return remote(
+            light_pages.at[2 * ci + lax.rem(cj, 2)], z_land.at[1, slot(other)], z_send.at[o],
+            z_recv.at[1, slot(other)], (tex, ci, cj),
         )
 
     def t_copy(o, slot):
@@ -281,18 +306,16 @@
             part.at[1], t_land.at[1, slot(other)], t_send.at[1, o], t_recv.at[1, slot(other)], (other, i, j)
         )
 
-    def last_copy(o, slot):
-        other = lax.rem(j + o, NV)
-        return remote(
-            whole.at[1], last_land.at[1, slot(other)], last_send.at[o], last_recv.at[1, slot(other)], (tex, i, other)
-        )
+    last_copy = remote(
+        whole.at[1], last_land.at[1, core], last_send.at[0], last_recv.at[1, 0], (tex, i, others[1])
+    )
 
     takes = j == x
 
     def vt_copy(o, slot):
         other = texel_at(o)
         return remote(
-            pages.at[0, other], t_land.at[0, slot(other)], t_send.at[0, o], t_recv.at[0, slot(other)], (other, i, j)
+            pages.at[other], t_land.at[0, slot(other)], t_send.at[0, o], t_recv.at[0, slot(other)], (other, i, j)
         )
 
     def vz_copy(o, slot):
@@ -322,11 +345,12 @@
 
     for g in range(2):
         keep_ref[g] = keep_table(g)
-        pick_ref[g] = pick_table(g)
-        gather_ref[g] = gather_table(g)
-    pages[0] = to_pages(0, products(stack_of(g) for g in range(NG)))
+    pick_ref[...] = pick_table(0)
+    gather_ref[...] = gather_table(0)
+    packed_pick_ref[...], packed_gather_ref[...] = packed_tables()
+    pages[...] = to_pages(products(stack_of(g) for g in range(NG)))
     start_all(vt_copy, t_order, tex)
-    t_land[0, tex] = pages[0, tex]
+    t_land[0, tex] = pages[tex]
 
     for o in (2, 3, 1):
         core_copy(o, j, mine).start()
@@ -337,14 +361,14 @@
     for g in range(NG):
         for k in range(NL):
             pltpu.make_async_copy(pieces.at[g, part_of(0), :], light_land.at[k, g], light_recv.at[g, k]).wait()
-    pages[1] = to_pages(1, products(
+    light_pages[...] = to_packed(products(
         jnp.concatenate(
             [light_land[k, g, 16 * m : 16 * m + 16, :] for k in range(NL) for g in range(NG)], axis=0
         )
         for m in range(PART // 16)
     ))
     start_all(z_copy, z_order, me)
-    z_land[1, me] = pages[1, me]
+    z_land[1, me] = light_pages[2 * i + core]
 
     wait_all(vt_copy, t_order)
     part[0] = jnp.sum(t_land[0], axis=0)
@@ -404,8 +428,8 @@
     sent_all(z_copy, z_order, me)
     wait_all(t_copy, t_order)
     whole[1] = jnp.sum(t_land[1], axis=0)
-    start_all(last_copy, (2, 1, 3), j)
-    last_land[1, j] = whole[1]
+    last_copy.start()
+    last_land[1, core] = whole[1]
 
     for q in range(4):
         @pl.when(jnp.logical_not(jnp.logical_and(takes, y == q)))
@@ -418,11 +442,14 @@
             vlast_copy(o, y).wait_send()
 
     sent_all(t_copy, t_order, tex)
-    wait_all(last_copy, (2, 1, 3))
-    for g in range(2):
+    for q in range(4):
+        gram_ref[0, 5 * q : 5 * q + 5, :] = last_land[0, q, 0:5, 0:80]
+    last_copy.wait()
+    for c in range(2):
+        gram_ref[1, 10 * c : 10 * c + 8, :] = last_land[1, c, :, 0:80]
         for q in range(4):
-            gram_ref[g, 5 * q : 5 * q + 5, :] = last_land[g, q, 0:5, 0:80]
-    sent_all(last_copy, (2, 1, 3), j)
+            at = 10 * c + 8 + q // 2
+            gram_ref[1, at : at + 1, 40 * (q % 2) : 40 * (q % 2) + 40] = last_land[1, c, q : q + 1, 80:120]
 
 
 def body(slab, basis):
@@ -445,8 +472,10 @@
             pltpu.VMEM(slab.shape, BF),
             pltpu.VMEM(basis.shape, BF),
             pltpu.VMEM((2, STACK, STACK), F32),
-            pltpu.VMEM((2, 8 * PAGES, STACK), BF),
-            pltpu.VMEM((2, STACK, 128), BF),
+            pltpu.VMEM((8 * PAGES, STACK), BF),
+            pltpu.VMEM((STACK, 128), BF),
+            pltpu.VMEM((3 * 64, STACK), BF),
+            pltpu.VMEM((3 * STACK, 128), BF),
             pltpu.VMEM((PIECE, PIECE), BF),
             pltpu.VMEM((NV * PART, STACK), BF),
             pltpu.VMEM((NV, ROWS, CB), BF),
@@ -456,7 +485,8 @@
             pltpu.VMEM((NG, NV * PART, CB), BF),
             pltpu.VMEM((NV, NG, PART, CB), BF),
             pltpu.VMEM((NL, NG, PART, CB), BF),
-            pltpu.VMEM((2, PAGES, 8, 128), F32),
+            pltpu.VMEM((PAGES, 8, 128), F32),
+            pltpu.VMEM((8, 8, 128), F32),
             pltpu.VMEM((2, PAGES, 8, 128), F32),
             pltpu.VMEM((2, 8, 128), F32),
             pltpu.VMEM((2, texels, 8, 128), F32),

time: 48.2 us -> 47.9 us (level)
  no operation moved by 1% of the time
where the time goes in v5:
time: 47.9 us; the launch traced here: 47.8 us
  Pallas kernels  45.7 us (95%)
  local copies, waits for them, and re-layouts  0.91 us (2%)
  between operations  0.64 us (1%)
  other arithmetic  0.61 us (1%)
    pallas_call x1, Pallas kernels, body(): pl.pallas_call(kernel, out_shape=(pltpu.VMEM((2, VB, 80), F32), pltpu.VME...  45.7 us

profile of v5, /device:TPU:1, one launch (start us, length us, event | category | flops | bytes accessed | tf_op | source)
XLA Modules:
  0.0 47.8 jit_solution(16037019938908624532)
XLA Ops:
  0.6 45.7 %shard_map.49 = (f32[2,20,80]{2,1,0:T(8,128)S(1)}, bf16[240,1024]{1,0:T(8,128)(2,1)S(1)}) custom-call(bf16[20,20,1024]{2,1,0:T(8,128)(2,1)} %slab_hbm.1, bf16[20,48]{1,0:T(8,128)(2,1)} %basis_hbm.1), custom_call_target="tpu_custom_call" | custom-call | tf_op jit(solution)/shard_map/pallas_call | solution.py:463
  46.3 0.6 %multiply_bitcast_fusion = (f32[20,80]{1,0:T(8,128)}, f32[20,80]{1,0:T(8,128)}) fusion(f32[2,20,80]{2,1,0:T(8,128)S(1)} %get-tuple-element.5), kind=kLoop, calls=%fused_computation | loop fusion | flops 3200 | bytes 25600 | tf_op jit(solution)/shard_map/mul | solution.py:503
  46.9 0.9 %reshape.13 = bf16[12,20,1024]{2,1,0:T(8,128)(2,1)} reshape(bf16[240,1024]{1,0:T(8,128)(2,1)S(1)} %get-tuple-element.6) | data formatting | bytes 983040 | tf_op jit(solution)/shard_map/reshape | solution.py:503

commit v6 on v5

--- a/solution.py
+++ b/solution.py
@@ -290,14 +290,19 @@
     def texel_at(o):
         return 4 * lax.rem(x + o // 4, 4) + lax.rem(y + o % 4, 4)
 
-    core = lax.rem(j, 2)
-
-    def z_copy(o, slot):
-        other = lax.rem(me + o, PAGES)
-        ci, cj = lax.div(other, NV), lax.rem(other, NV)
-        return remote(
-            light_pages.at[2 * ci + lax.rem(cj, 2)], z_land.at[1, slot(other)], z_send.at[o],
-            z_recv.at[1, slot(other)], (tex, ci, cj),
+    sums = jnp.logical_or(j == 0, j == 3)
+    core = lax.div(j, 2)
+
+    def z_copy(d, c):
+        ci = lax.rem(i + d, NL)
+        return remote(
+            light_pages.at[2 * ci + c], z_land.at[1, me], z_send.at[2 * d + c], z_recv.at[1, me], (tex, ci, 3 * c)
+        )
+
+    def z_landed(o):
+        source = lax.rem(me + o, PAGES)
+        return remote(
+            light_pages.at[0], z_land.at[1, source], z_send.at[0], z_recv.at[1, source], (tex, i, others[1])
         )
 
     def t_copy(o, slot):
@@ -306,9 +311,15 @@
             part.at[1], t_land.at[1, slot(other)], t_send.at[1, o], t_recv.at[1, slot(other)], (other, i, j)
         )
 
-    last_copy = remote(
-        whole.at[1], last_land.at[1, core], last_send.at[0], last_recv.at[1, 0], (tex, i, others[1])
-    )
+    def last_copy(o):
+        return remote(
+            whole.at[1], last_land.at[1, core], last_send.at[o], last_recv.at[1, core], (tex, i, others[o])
+        )
+
+    def last_landed(c):
+        return remote(
+            whole.at[1], last_land.at[1, c], last_send.at[1], last_recv.at[1, c], (tex, i, others[1])
+        )
 
     takes = j == x
 
@@ -367,8 +378,18 @@
         )
         for m in range(PART // 16)
     ))
-    start_all(z_copy, z_order, me)
-    z_land[1, me] = light_pages[2 * i + core]
+    for d in (2, 1, 3):
+        for c in range(2):
+            z_copy(d, c).start()
+    for c in range(2):
+        @pl.when(j == 3 * c)
+        def _():
+            z_land[1, me] = light_pages[2 * i + c]
+
+        @pl.when(j != 3 * c)
+        def _():
+            z_copy(0, c).start()
+
 
     wait_all(vt_copy, t_order)
     part[0] = jnp.sum(t_land[0], axis=0)
@@ -396,11 +417,6 @@
                 light_copy(g, o, ci, cj).wait_send()
 
     sent_all(vt_copy, t_order, tex)
-    wait_all(z_copy, z_order)
-    part[1] = jnp.sum(z_land[1], axis=0)
-    start_all(t_copy, t_order, tex)
-    t_land[1, tex] = part[1]
-
     @pl.when(takes)
     def _():
         for o in z_order:
@@ -409,6 +425,14 @@
         for o in t_order:
             vlast_copy(o, y).start()
         last_land[0, y] = whole[0]
+
+    @pl.when(sums)
+    def _():
+        for o in z_order:
+            z_landed(o).wait_recv()
+        part[1] = jnp.sum(z_land[1], axis=0)
+        start_all(t_copy, t_order, tex)
+        t_land[1, tex] = part[1]
 
     own_piece.wait()
     for o in (1, 2, 3):
@@ -425,11 +449,21 @@
     def _():
         vz_copy(0, me).wait_send()
 
-    sent_all(z_copy, z_order, me)
-    wait_all(t_copy, t_order)
-    whole[1] = jnp.sum(t_land[1], axis=0)
-    last_copy.start()
-    last_land[1, core] = whole[1]
+    for d in (2, 1, 3):
+        for c in range(2):
+            z_copy(d, c).wait_send()
+    for c in range(2):
+        @pl.when(j != 3 * c)
+        def _():
+            z_copy(0, c).wait_send()
+
+    @pl.when(sums)
+    def _():
+        wait_all(t_copy, t_order)
+        whole[1] = jnp.sum(t_land[1], axis=0)
+        for o in (2, 3, 1):
+            last_copy(o).start()
+        last_land[1, core] = whole[1]
 
     for q in range(4):
         @pl.when(jnp.logical_not(jnp.logical_and(takes, y == q)))
@@ -441,10 +475,22 @@
         for o in t_order:
             vlast_copy(o, y).wait_send()
 
-    sent_all(t_copy, t_order, tex)
+    @pl.when(sums)
+    def _():
+        sent_all(t_copy, t_order, tex)
+
     for q in range(4):
         gram_ref[0, 5 * q : 5 * q + 5, :] = last_land[0, q, 0:5, 0:80]
-    last_copy.wait()
+    for c in range(2):
+        @pl.when(j != 3 * c)
+        def _():
+            last_landed(c).wait_recv()
+
+    @pl.when(sums)
+    def _():
+        for o in (2, 3, 1):
+            last_copy(o).wait_send()
+
     for c in range(2):
         gram_ref[1, 10 * c : 10 * c + 8, :] = last_land[1, c, :, 0:80]
         for q in range(4):

time: 47.9 us -> 47.3 us (0.987)
  Pallas kernels: 45.7 us -> 45 us
    pallas_call x1, Pallas kernels: 45.7 us -> 45 us  [body(): pl.pallas_call(kernel, out_shape=(pltpu.VMEM((2, VB, 80), F32), pltpu.VME...]
where the time goes in v6:
time: 47.3 us; the launch traced here: 47.2 us
  Pallas kernels  45 us (95%)
  local copies, waits for them, and re-layouts  0.91 us (2%)
  between operations  0.64 us (1%)
  other arithmetic  0.61 us (1%)
    pallas_call x1, Pallas kernels, body(): pl.pallas_call(kernel, out_shape=(pltpu.VMEM((2, VB, 80), F32), pltpu.VME...  45 us

profile of v6, /device:TPU:1, one launch (start us, length us, event | category | flops | bytes accessed | tf_op | source)
XLA Modules:
  0.0 47.2 jit_solution(12470156562826763401)
XLA Ops:
  0.6 45.0 %shard_map.49 = (f32[2,20,80]{2,1,0:T(8,128)S(1)}, bf16[240,1024]{1,0:T(8,128)(2,1)S(1)}) custom-call(bf16[20,20,1024]{2,1,0:T(8,128)(2,1)} %slab_hbm.1, bf16[20,48]{1,0:T(8,128)(2,1)} %basis_hbm.1), custom_call_target="tpu_custom_call" | custom-call | tf_op jit(solution)/shard_map/pallas_call | solution.py:509
  45.7 0.6 %multiply_bitcast_fusion = (f32[20,80]{1,0:T(8,128)}, f32[20,80]{1,0:T(8,128)}) fusion(f32[2,20,80]{2,1,0:T(8,128)S(1)} %get-tuple-element.5), kind=kLoop, calls=%fused_computation | loop fusion | flops 3200 | bytes 25600 | tf_op jit(solution)/shard_map/mul | solution.py:549
  46.3 0.9 %reshape.13 = bf16[12,20,1024]{2,1,0:T(8,128)(2,1)} reshape(bf16[240,1024]{1,0:T(8,128)(2,1)S(1)} %get-tuple-element.6) | data formatting | bytes 983040 | tf_op jit(solution)/shard_map/reshape | solution.py:549

commit v7 on v6

--- a/solution.py
+++ b/solution.py
@@ -19,7 +19,7 @@
 NG = 5
 GROUP = 4 * VB
 STACK = NV * GROUP
-AHEAD = 3
+AHEAD = 4
 PART = 4 * RB
 PAGES = NL * NV
 
@@ -157,19 +157,16 @@
         copy.start()
     barrier = pltpu.get_barrier_semaphore()
 
-    def greet_z(o, c):
-        other = lax.rem(me + o, PAGES)
-        pl.semaphore_signal(
-            barrier, inc=1, device_id=(tex, lax.div(other, NV), lax.rem(other, NV)), device_id_type=MESH
-        )
-        return c
-
-    def greet_t(o, c):
-        pl.semaphore_signal(barrier, inc=1, device_id=(lax.rem(tex + o, texels), i, j), device_id_type=MESH)
-        return c
-
-    lax.fori_loop(1, PAGES, greet_z, 0)
-    lax.fori_loop(1, texels, greet_t, 0)
+    def greet(device):
+        pl.semaphore_signal(barrier, inc=1, device_id=device, device_id_type=MESH)
+
+    for o in (1, 2, 3):
+        greet((tex, i, lax.rem(j + o, NV)))
+    for d in (2, 1, 3):
+        for o in range(NV):
+            greet((tex, lax.rem(i + d, NL), o))
+    for o in range(1, texels):
+        greet((lax.rem(tex + o, texels), i, j))
 
     own_basis[...] = jnp.zeros_like(own_basis)
     load_basis.wait()

time: 47.3 us -> 46.6 us (0.985)
  Pallas kernels: 45 us -> 44.3 us
    pallas_call x1, Pallas kernels: 45 us -> 44.3 us  [body(): pl.pallas_call(kernel, out_shape=(pltpu.VMEM((2, VB, 80), F32), pltpu.VME...]
where the time goes in v7:
time: 46.6 us; the launch traced here: 46.4 us
  Pallas kernels  44.3 us (95%)
  local copies, waits for them, and re-layouts  0.91 us (2%)
  between operations  0.64 us (1%)
  other arithmetic  0.61 us (1%)
    pallas_call x1, Pallas kernels, body(): pl.pallas_call(kernel, out_shape=(pltpu.VMEM((2, VB, 80), F32), pltpu.VME...  44.3 us

profile of v7, /device:TPU:1, one launch (start us, length us, event | category | flops | bytes accessed | tf_op | source)
XLA Modules:
  0.0 46.4 jit_solution(15569418457119439200)
XLA Ops:
  0.6 44.3 %shard_map.49 = (f32[2,20,80]{2,1,0:T(8,128)S(1)}, bf16[240,1024]{1,0:T(8,128)(2,1)S(1)}) custom-call(bf16[20,20,1024]{2,1,0:T(8,128)(2,1)} %slab_hbm.1, bf16[20,48]{1,0:T(8,128)(2,1)} %basis_hbm.1), custom_call_target="tpu_custom_call" | custom-call | tf_op jit(solution)/shard_map/pallas_call | solution.py:506
  44.9 0.6 %multiply_bitcast_fusion = (f32[20,80]{1,0:T(8,128)}, f32[20,80]{1,0:T(8,128)}) fusion(f32[2,20,80]{2,1,0:T(8,128)S(1)} %get-tuple-element.5), kind=kLoop, calls=%fused_computation | loop fusion | flops 3200 | bytes 25600 | tf_op jit(solution)/shard_map/mul | solution.py:546
  45.5 0.9 %reshape.13 = bf16[12,20,1024]{2,1,0:T(8,128)(2,1)} reshape(bf16[240,1024]{1,0:T(8,128)(2,1)S(1)} %get-tuple-element.6) | data formatting | bytes 983040 | tf_op jit(solution)/shard_map/reshape | solution.py:546

commit v8 on v7

--- a/solution.py
+++ b/solution.py
@@ -414,6 +414,14 @@
                 light_copy(g, o, ci, cj).wait_send()
 
     sent_all(vt_copy, t_order, tex)
+    @pl.when(sums)
+    def _():
+        for o in z_order:
+            z_landed(o).wait_recv()
+        part[1] = jnp.sum(z_land[1], axis=0)
+        start_all(t_copy, t_order, tex)
+        t_land[1, tex] = part[1]
+
     @pl.when(takes)
     def _():
         for o in z_order:
@@ -422,14 +430,6 @@
         for o in t_order:
             vlast_copy(o, y).start()
         last_land[0, y] = whole[0]
-
-    @pl.when(sums)
-    def _():
-        for o in z_order:
-            z_landed(o).wait_recv()
-        part[1] = jnp.sum(z_land[1], axis=0)
-        start_all(t_copy, t_order, tex)
-        t_land[1, tex] = part[1]
 
     own_piece.wait()
     for o in (1, 2, 3):

time: 46.6 us -> 46.6 us (level)
  no operation moved by 1% of the time
where the time goes in v8:
time: 46.6 us; the launch traced here: 46.4 us
  Pallas kernels  44.3 us (95%)
  local copies, waits for them, and re-layouts  0.91 us (2%)
  between operations  0.64 us (1%)
  other arithmetic  0.61 us (1%)
    pallas_call x1, Pallas kernels, body(): pl.pallas_call(kernel, out_shape=(pltpu.VMEM((2, VB, 80), F32), pltpu.VME...  44.3 us

profile of v8, /device:TPU:1, one launch (start us, length us, event | category | flops | bytes accessed | tf_op | source)
XLA Modules:
  0.0 46.4 jit_solution(7221677514725181453)
XLA Ops:
  0.6 44.3 %shard_map.49 = (f32[2,20,80]{2,1,0:T(8,128)S(1)}, bf16[240,1024]{1,0:T(8,128)(2,1)S(1)}) custom-call(bf16[20,20,1024]{2,1,0:T(8,128)(2,1)} %slab_hbm.1, bf16[20,48]{1,0:T(8,128)(2,1)} %basis_hbm.1), custom_call_target="tpu_custom_call" | custom-call | tf_op jit(solution)/shard_map/pallas_call | solution.py:506
  44.9 0.6 %multiply_bitcast_fusion = (f32[20,80]{1,0:T(8,128)}, f32[20,80]{1,0:T(8,128)}) fusion(f32[2,20,80]{2,1,0:T(8,128)S(1)} %get-tuple-element.5), kind=kLoop, calls=%fused_computation | loop fusion | flops 3200 | bytes 25600 | tf_op jit(solution)/shard_map/mul | solution.py:546
  45.5 0.9 %reshape.13 = bf16[12,20,1024]{2,1,0:T(8,128)(2,1)} reshape(bf16[240,1024]{1,0:T(8,128)(2,1)S(1)} %get-tuple-element.6) | data formatting | bytes 983040 | tf_op jit(solution)/shard_map/reshape | solution.py:546
